TPU v7x, 256 devices: a whole 4x4x8 slice. The times are simulated.
256 devices in a mesh: expert: 32 (over x, y, core), dp: 8 (over z).
Axes of the slice: x: 4, y: 4, z: 8, core: 2. Of those that a mesh axis runs over, the one named last changes fastest.
Arguments:
- tokens: bfloat16 [8192, 2048], P(('expert', 'dp')), may hold values from -6 to 6
- upstream: bfloat16 [8192, 2048], P(('expert', 'dp')), may hold values from -4 to 4
- gate_probs: bfloat16 [8192, 8], P(('expert', 'dp')), may hold values from 0.19921875 to 1
- routes: int32 [8192, 8], P(('expert', 'dp')), may hold values from 0 to 127, all different within a row; in each aligned block of 32 rows (0 to 31, 32 to 63, ...) at most 2 rows name the same one
- w_gate: bfloat16 [256, 2048, 384], P(('expert', 'dp')), may hold values from -0.125 to 0.125
- w_up: bfloat16 [256, 2048, 384], P(('expert', 'dp')), may hold values from -0.125 to 0.125
- w_down: bfloat16 [256, 384, 2048], P(('expert', 'dp')), may hold values from -0.21875 to 0.21875
Outputs:
- input_grad: bfloat16 [8192, 2048], P(('expert', 'dp'))
- gate_prob_grad: float32 [8192, 8], P(('expert', 'dp'))
- gate_weight_grad: bfloat16 [256, 2048, 384], P(('expert', 'dp'))
- up_weight_grad: bfloat16 [256, 2048, 384], P(('expert', 'dp'))
- down_weight_grad: bfloat16 [256, 384, 2048], P(('expert', 'dp'))
Inputs may be any that keep to these rules, and one draw needn't show every extreme that they name: `routes`: each row names 8 different experts. Among the rows of one device no expert is named more than 2 times, a bound that some block reaches; every expert is named somewhere.
All inputs are finite; a program needn't handle non-finite values.
Results may differ from a plain program's by a relative error of at most 0.0095.
Values may be sent and summed in bfloat16 or wider, within the bound.
A program may use at most 128 MiB of HBM per device.

v0:
```python
import jax
import jax.numpy as jnp
from jax import lax
from jax.sharding import PartitionSpec as P


def silu_parts(pre_gate):
    sigmoid = jax.nn.sigmoid(pre_gate)
    return (pre_gate * sigmoid, sigmoid * (1.0 + pre_gate * (1.0 - sigmoid)))


def doubled(block):
    shape_in = block.shape
    spread = jnp.broadcast_to(block[:, :, None], shape_in[:2] + (2,) + shape_in[2:])
    return spread.reshape((shape_in[0], shape_in[1] * 2) + shape_in[2:])


def local(tokens, upstream, gate_probs, routes, w_gate, w_up, w_down):
    column_count = lax.axis_size("expert")
    row_count = lax.axis_size("dp")
    token_count, model_width = tokens.shape
    top_count = routes.shape[1]
    experts = column_count * row_count // 2
    capacity = min(token_count, max(2, 5 * token_count * top_count // (4 * experts)))
    contract_rows = (((0,), (0,)), ((), ()))
    contract_cols = (((1,), (1,)), ((), ()))
    flat_expert = routes.reshape(-1)
    onehot = (flat_expert[:, None] == jnp.arange(experts, dtype=jnp.int32)[None, :]).astype(
        jnp.int32
    )
    position = jnp.sum((jnp.cumsum(onehot, axis=0) - onehot) * onehot, axis=1)
    slot_index = flat_expert * capacity + position
    route_token = jnp.arange(token_count * top_count, dtype=jnp.int32) // top_count
    slot_token = (
        jnp.full((experts * capacity,), token_count, jnp.int32).at[slot_index].set(route_token)
    )
    slot_prob = (
        jnp.zeros((experts * capacity,), jnp.bfloat16).at[slot_index].set(gate_probs.reshape(-1))
    )
    zero_row = jnp.zeros((1, model_width), jnp.bfloat16)
    send_shape = (column_count, row_count // 2, capacity, model_width)
    send_rows = jnp.concatenate([tokens, zero_row], axis=0)[slot_token].reshape(send_shape)
    send_grads = jnp.concatenate([upstream, zero_row], axis=0)[slot_token].reshape(send_shape)
    send_probs = slot_prob.reshape(send_shape[:3])
    by_column = (
        lax.all_to_all(send_rows, "expert", split_axis=0, concat_axis=0, tiled=True),
        lax.all_to_all(send_grads, "expert", split_axis=0, concat_axis=0, tiled=True),
        lax.all_to_all(send_probs, "expert", split_axis=0, concat_axis=0, tiled=True),
    )
    arrived = (
        lax.all_to_all(doubled(by_column[0]), "dp", split_axis=1, concat_axis=1, tiled=True),
        lax.all_to_all(doubled(by_column[1]), "dp", split_axis=1, concat_axis=1, tiled=True),
        lax.all_to_all(doubled(by_column[2]), "dp", split_axis=1, concat_axis=1, tiled=True),
    )
    recv_shape = arrived[0].shape
    routed_rows = arrived[0].reshape(-1, model_width)
    routed_grads = arrived[1].reshape(-1, model_width)
    routed_probs = arrived[2].reshape(-1, 1).astype(jnp.float32)
    scaled = (routed_probs * routed_grads.astype(jnp.float32)).astype(jnp.bfloat16)
    gate_local = w_gate[0]
    up_local = w_up[0]
    down_local = w_down[0]
    pre_gate = jnp.dot(routed_rows, gate_local, preferred_element_type=jnp.float32)
    pre_up = jnp.dot(routed_rows, up_local, preferred_element_type=jnp.float32)
    activation, derivative = silu_parts(pre_gate)
    hidden = (activation * pre_up).astype(jnp.bfloat16)
    back_proj = lax.dot_general(
        routed_grads, down_local, contract_cols, preferred_element_type=jnp.float32
    )
    partial_value = jnp.sum(hidden.astype(jnp.float32) * back_proj, axis=1)
    grad_hidden = routed_probs * back_proj
    gate_delta = (grad_hidden * pre_up * derivative).astype(jnp.bfloat16)
    up_delta = (grad_hidden * activation).astype(jnp.bfloat16)
    gate_weight_grad = lax.dot_general(
        routed_rows, gate_delta, contract_rows, preferred_element_type=jnp.float32
    ).astype(jnp.bfloat16)[None]
    up_weight_grad = lax.dot_general(
        routed_rows, up_delta, contract_rows, preferred_element_type=jnp.float32
    ).astype(jnp.bfloat16)[None]
    down_weight_grad = lax.dot_general(
        hidden, scaled, contract_rows, preferred_element_type=jnp.float32
    ).astype(jnp.bfloat16)[None]
    half_term = lax.dot_general(
        gate_delta, gate_local, contract_cols, preferred_element_type=jnp.float32
    ) + lax.dot_general(up_delta, up_local, contract_cols, preferred_element_type=jnp.float32)
    term_blocks = half_term.reshape(recv_shape)
    partial_blocks = partial_value.reshape(recv_shape[:3])
    token_match = (
        slot_token.reshape(experts, capacity)[None]
        == jnp.arange(token_count, dtype=jnp.int32)[:, None, None]
    ).astype(jnp.bfloat16)
    row_back = (
        lax.all_to_all(term_blocks, "dp", split_axis=1, concat_axis=1, tiled=True),
        lax.all_to_all(partial_blocks, "dp", split_axis=1, concat_axis=1, tiled=True),
    )
    returned = (
        lax.all_to_all(row_back[0], "expert", split_axis=0, concat_axis=0, tiled=True),
        lax.all_to_all(row_back[1], "expert", split_axis=0, concat_axis=0, tiled=True),
    )
    terms = returned[0].reshape(experts, 2, capacity, model_width)
    partials = returned[1].reshape(experts, 2, capacity)
    route_term = (terms[:, 0] + terms[:, 1]).astype(jnp.bfloat16)
    route_partial = (partials[:, 0] + partials[:, 1]).astype(jnp.bfloat16)
    input_grad = jnp.einsum(
        "tec,ecd->td", token_match, route_term, preferred_element_type=jnp.float32
    ).astype(jnp.bfloat16)
    summed = route_partial.astype(jnp.float32).reshape(-1)
    gate_prob_grad = summed[slot_index].reshape(token_count, top_count)
    return (input_grad, gate_prob_grad, gate_weight_grad, up_weight_grad, down_weight_grad)


def solution(mesh):
    in_specs = (
        P(("expert", "dp"), None),
        P(("expert", "dp"), None),
        P(("expert", "dp"), None),
        P(("expert", "dp"), None),
        P(("expert", "dp"), None, None),
        P(("expert", "dp"), None, None),
        P(("expert", "dp"), None, None),
    )
    out_specs = (
        P(("expert", "dp"), None),
        P(("expert", "dp"), None),
        P(("expert", "dp"), None, None),
        P(("expert", "dp"), None, None),
        P(("expert", "dp"), None, None),
    )
    return jax.shard_map(local, mesh=mesh, in_specs=in_specs, out_specs=out_specs, check_vma=False)
```

profile of v0, /device:TPU:1, one launch (start us, length us, event | category | flops | bytes accessed | tf_op | source)
XLA Modules:
  0.0 414.7 jit_solution(5664889446921554202)
XLA Ops:
  0.6 0.8 broadcast_multiply_fusion
  1.5 0.8 copy.86
  2.4 0.8 copy.91
  3.5 0.2 fusion.18
  3.9 0.2 fusion.20
  4.0 2.2 scatter_custom_fusion.1
  6.2 0.2 reshape.123
  6.4 0.9 copy.92
  7.3 8.6 %all-to-all-start = ((bf16[32,4,2]{1,2,0:T(2,128)(2,1)}), bf16[32,4,2]{1,2,0:T(2,128)(2,1)S(1)}, u32[]{:S(2)}, u32[]{:S(2)}) async-start(bf16[32,4,2]{1,2,0:T(2,128)(2,1)} %copy.92), calls=%async_computation | async-start | bytes 32768 | tf_op jit(solution)/shard_map/all_to_all | solution.py:48
  15.9 1.4 scatter_custom_fusion
  17.3 5.4 %all-to-all-done = bf16[32,4,2]{1,2,0:T(2,128)(2,1)S(1)} async-done(((bf16[32,4,2]{1,2,0:T(2,128)(2,1)}), bf16[32,4,2]{1,2,0:T(2,128)(2,1)S(1)}, u32[]{:S(2)}, u32[]{:S(2)}) %all-to-all-start) | async-done | bytes 544 | tf_op jit(solution)/shard_map/all_to_all | solution.py:48
  22.9 0.6 broadcast_in_dim.20
  23.5 8.2 %all-to-all-start.1 = ((bf16[32,8,2]{0,2,1:T(2,128)(2,1)}), bf16[32,8,2]{0,2,1:T(2,128)(2,1)S(1)}, u32[]{:S(2)}, u32[]{:S(2)}) async-start(bf16[32,8,2]{0,2,1:T(2,128)(2,1)} %bitcast.5), calls=%async_computation.1 | async-start | bytes 8192 | tf_op jit(solution)/shard_map/all_to_all | solution.py:53
  31.7 0.9 concatenate.7
  32.6 1.4 gather_fusion.1
  34.0 1.5 reshape.128
  35.5 2.6 all-to-all-done.1
  38.1 6.3 %all-to-all-start.4 = ((bf16[32,4,2,2048]{3,2,1,0:T(2,128)(2,1)}), bf16[32,4,2,2048]{3,2,1,0:T(2,128)(2,1)}, u32[]{:S(2)}, u32[]{:S(2)}) async-start(bf16[32,4,2,2048]{3,2,1,0:T(2,128)(2,1)} %reshape.128), calls=%async_computation.4 | async-start | bytes 2097152 | tf_op jit(solution)/shard_map/all_to_all | solution.py:46
  44.5 1.4 gather_fusion
  45.8 1.5 reshape.125
  47.3 14.2 %all-to-all-done.4 = bf16[32,4,2,2048]{3,2,1,0:T(2,128)(2,1)} async-done(((bf16[32,4,2,2048]{3,2,1,0:T(2,128)(2,1)}), bf16[32,4,2,2048]{3,2,1,0:T(2,128)(2,1)}, u32[]{:S(2)}, u32[]{:S(2)}) %all-to-all-start.4) | async-done | bytes 1048608 | tf_op jit(solution)/shard_map/all_to_all | solution.py:46
  61.5 4.5 %all-to-all-start.2 = ((bf16[32,4,2,2048]{3,2,1,0:T(2,128)(2,1)}), bf16[32,4,2,2048]{3,2,1,0:T(2,128)(2,1)}, u32[]{:S(2)}, u32[]{:S(2)}) async-start(bf16[32,4,2,2048]{3,2,1,0:T(2,128)(2,1)} %reshape.125), calls=%async_computation.2 | async-start | bytes 2097152 | tf_op jit(solution)/shard_map/all_to_all | solution.py:47
  66.0 2.0 copy.98
  68.0 15.0 %all-to-all-done.2 = bf16[32,4,2,2048]{3,2,1,0:T(2,128)(2,1)} async-done(((bf16[32,4,2,2048]{3,2,1,0:T(2,128)(2,1)}), bf16[32,4,2,2048]{3,2,1,0:T(2,128)(2,1)}, u32[]{:S(2)}, u32[]{:S(2)}) %all-to-all-start.2) | async-done | bytes 1048608 | tf_op jit(solution)/shard_map/all_to_all | solution.py:47
  83.0 2.8 broadcast_in_dim.23
  85.8 4.4 %all-to-all-start.5 = ((bf16[32,8,2,2048]{3,2,0,1:T(2,128)(2,1)}), bf16[32,8,2,2048]{3,2,0,1:T(2,128)(2,1)}, u32[]{:S(2)}, u32[]{:S(2)}) async-start(bf16[32,8,2,2048]{3,2,0,1:T(2,128)(2,1)} %bitcast.63), calls=%async_computation.5 | async-start | bytes 4194304 | tf_op jit(solution)/shard_map/all_to_all | solution.py:51
  90.1 2.0 copy.96
  92.2 46.2 %all-to-all-done.5 = bf16[32,8,2,2048]{3,2,0,1:T(2,128)(2,1)} async-done(((bf16[32,8,2,2048]{3,2,0,1:T(2,128)(2,1)}), bf16[32,8,2,2048]{3,2,0,1:T(2,128)(2,1)}, u32[]{:S(2)}, u32[]{:S(2)}) %all-to-all-start.5) | async-done | bytes 2097184 | tf_op jit(solution)/shard_map/all_to_all | solution.py:51
  138.4 2.8 broadcast_in_dim.22
  141.2 4.9 %all-to-all-start.3 = ((bf16[32,8,2,2048]{3,2,0,1:T(2,128)(2,1)}), bf16[32,8,2,2048]{3,2,0,1:T(2,128)(2,1)}, u32[]{:S(2)}, u32[]{:S(2)}) async-start(bf16[32,8,2,2048]{3,2,0,1:T(2,128)(2,1)} %bitcast.62), calls=%async_computation.3 | async-start | bytes 4194304 | tf_op jit(solution)/shard_map/all_to_all | solution.py:52
  146.1 0.1 copy.95
  146.3 0.1 reshape.136
  146.4 5.2 %copy.99 = bf16[32,8,2,2048]{3,2,1,0:T(2,128)(2,1)} copy(bf16[32,8,2,2048]{3,2,0,1:T(2,128)(2,1)} %all-to-all-done.5) | data formatting | bytes 4194304 | tf_op jit(solution)/shard_map/all_to_all | solution.py:51
  151.6 4.2 %reshape.130 = bf16[512,2048]{1,0:T(8,128)(2,1)} reshape(bf16[32,8,2,2048]{3,2,1,0:T(2,128)(2,1)} %copy.99) | data formatting | bytes 4194304 | tf_op jit(solution)/shard_map/reshape | solution.py:56
  155.8 3.6 fusion.8
  159.4 1.9 fusion.11
  161.4 34.0 %all-to-all-done.3 = bf16[32,8,2,2048]{3,2,0,1:T(2,128)(2,1)} async-done(((bf16[32,8,2,2048]{3,2,0,1:T(2,128)(2,1)}), bf16[32,8,2,2048]{3,2,0,1:T(2,128)(2,1)}, u32[]{:S(2)}, u32[]{:S(2)}) %all-to-all-start.3) | async-done | bytes 2097184 | tf_op jit(solution)/shard_map/all_to_all | solution.py:52
  195.4 5.2 %copy.97 = bf16[32,8,2,2048]{3,2,1,0:T(2,128)(2,1)} copy(bf16[32,8,2,2048]{3,2,0,1:T(2,128)(2,1)} %all-to-all-done.3) | data formatting | bytes 4194304 | tf_op jit(solution)/shard_map/all_to_all | solution.py:52
  200.5 4.1 reshape.127
  204.7 4.7 %multiply_reduce_fusion = (f32[512]{0:T(512)S(1)}, bf16[512,384]{0,1:T(8,128)(2,1)}, bf16[512,384]{0,1:T(8,128)(2,1)S(1)}, bf16[512,384]{0,1:T(8,128)(2,1)}) fusion(f32[512,384]{0,1:T(8,128)} %fusion.11, f32[512,384]{0,1:T(8,128)} %fusion.8, f32[512]{0:T(512)S(1)} %reshape.136, bf16[512,2048]{1,0:T(8,128)(2,1)} %reshape.127, bf16[1,384,2048]{2,1,0:T(8,128)(2,1)} %param.13), kind=kOutput, calls=%fused_computation.29 | convolution fusion | flops 809041408 | bytes 6426624 | tf_op jit(solution)/shard_map/dot_general | solution.py:67
  209.4 0.8 reshape.133
  210.2 1.6 copy.103
  211.8 3.6 all-to-all-start.8
  215.4 1.3 fusion.6
  216.7 3.3 convolution_add_fusion
  220.0 5.8 %reshape.131 = f32[32,8,2,2048]{3,2,1,0:T(2,128)} reshape(f32[512,2048]{1,0:T(8,128)} %convolution_add_fusion) | data formatting | bytes 8388608 | tf_op jit(solution)/shard_map/reshape | solution.py:86
  225.9 6.8 %copy.100 = f32[32,8,2,2048]{3,2,0,1:T(2,128)} copy(f32[32,8,2,2048]{3,2,1,0:T(2,128)} %reshape.131) | data formatting | bytes 8388608 | tf_op jit(solution)/shard_map/reshape | solution.py:86
  232.7 6.3 %all-to-all-start.6 = ((f32[32,8,2,2048]{3,2,0,1:T(2,128)}), f32[32,8,2,2048]{3,2,0,1:T(2,128)}, u32[]{:S(2)}, u32[]{:S(2)}) async-start(f32[32,8,2,2048]{3,2,0,1:T(2,128)} %copy.100), calls=%async_computation.6 | async-start | bytes 8388608 | tf_op jit(solution)/shard_map/all_to_all | solution.py:93
  239.0 0.7 copy.104
  239.7 91.8 %all-to-all-done.6 = f32[32,8,2,2048]{3,2,0,1:T(2,128)} async-done(((f32[32,8,2,2048]{3,2,0,1:T(2,128)}), f32[32,8,2,2048]{3,2,0,1:T(2,128)}, u32[]{:S(2)}, u32[]{:S(2)}) %all-to-all-start.6) | async-done | bytes 4194336 | tf_op jit(solution)/shard_map/all_to_all | solution.py:93
  331.5 11.9 %all-to-all-start.9 = ((f32[32,8,2]{1,2,0:T(2,128)}), f32[32,8,2]{1,2,0:T(2,128)S(1)}, u32[]{:S(2)}, u32[]{:S(2)}) async-start(f32[32,8,2]{1,2,0:T(2,128)} %copy.104), calls=%async_computation.9 | async-start | bytes 65536 | tf_op jit(solution)/shard_map/all_to_all | solution.py:98
  343.4 6.9 %copy.101 = f32[32,8,2,2048]{3,2,1,0:T(2,128)} copy(f32[32,8,2,2048]{3,2,0,1:T(2,128)} %all-to-all-done.6) | data formatting | bytes 8388608 | tf_op jit(solution)/shard_map/all_to_all | solution.py:93
  350.3 0.4 all-to-all-done.9
  350.7 7.1 %all-to-all-start.7 = ((f32[32,8,2,2048]{3,2,1,0:T(2,128)}), f32[32,8,2,2048]{3,2,1,0:T(2,128)}, u32[]{:S(2)}, u32[]{:S(2)}) async-start(f32[32,8,2,2048]{3,2,1,0:T(2,128)} %copy.101), calls=%async_computation.7 | async-start | bytes 8388608 | tf_op jit(solution)/shard_map/all_to_all | solution.py:97
  357.8 0.1 eq.48
  358.0 4.2 %fusion = bf16[1,2048,384]{2,1,0:T(8,128)(2,1)} fusion(bf16[512,2048]{1,0:T(8,128)(2,1)} %reshape.130, bf16[512,384]{0,1:T(8,128)(2,1)S(1)} %get-tuple-element.32), kind=kOutput, calls=%fused_computation.10 | convolution fusion | flops 806092800 | bytes 4063232 | tf_op jit(solution)/shard_map/dot_general | solution.py:74
  362.3 2.5 fusion.1
  364.7 2.3 fusion.2
  367.5 0.1 reshape.137
  367.7 1.9 gather_fusion.2
  369.7 0.7 copy.109
  370.4 39.6 %all-to-all-done.7 = f32[32,8,2,2048]{3,2,1,0:T(2,128)} async-done(((f32[32,8,2,2048]{3,2,1,0:T(2,128)}), f32[32,8,2,2048]{3,2,1,0:T(2,128)}, u32[]{:S(2)}, u32[]{:S(2)}) %all-to-all-start.7) | async-done | bytes 4194336 | tf_op jit(solution)/shard_map/all_to_all | solution.py:97
  410.0 3.4 fusion.16
  413.4 1.3 fusion.3
  (54 shorter events, 1.5 us)
Async XLA Ops:
  0.6 155.2 %copy-start = (bf16[1,2048,384]{2,1,0:T(8,128)(2,1)S(1)}, bf16[1,2048,384]{2,1,0:T(8,128)(2,1)}, u32[]{:S(2)}) copy-start(bf16[1,2048,384]{2,1,0:T(8,128)(2,1)} %param.11) | copy-start | bytes 4718596
  7.3 15.5 %all-to-all-start = ((bf16[32,4,2]{1,2,0:T(2,128)(2,1)}), bf16[32,4,2]{1,2,0:T(2,128)(2,1)S(1)}, u32[]{:S(2)}, u32[]{:S(2)}) async-start(bf16[32,4,2]{1,2,0:T(2,128)(2,1)} %copy.92), calls=%async_computation | async-start | bytes 32768 | tf_op jit(solution)/shard_map/all_to_all | solution.py:48
  23.5 14.6 %all-to-all-start.1 = ((bf16[32,8,2]{0,2,1:T(2,128)(2,1)}), bf16[32,8,2]{0,2,1:T(2,128)(2,1)S(1)}, u32[]{:S(2)}, u32[]{:S(2)}) async-start(bf16[32,8,2]{0,2,1:T(2,128)(2,1)} %bitcast.5), calls=%async_computation.1 | async-start | bytes 8192 | tf_op jit(solution)/shard_map/all_to_all | solution.py:53
  33.9 10.5 %copy-start.8 = (bf16[32,2048]{1,0:T(8,128)(2,1)S(1)}, bf16[32,2048]{1,0:T(8,128)(2,1)}, u32[]{:S(2)}) copy-start(bf16[32,2048]{1,0:T(8,128)(2,1)} %param.8) | copy-start | bytes 393220
  38.1 23.4 %all-to-all-start.4 = ((bf16[32,4,2,2048]{3,2,1,0:T(2,128)(2,1)}), bf16[32,4,2,2048]{3,2,1,0:T(2,128)(2,1)}, u32[]{:S(2)}, u32[]{:S(2)}) async-start(bf16[32,4,2,2048]{3,2,1,0:T(2,128)(2,1)} %reshape.128), calls=%async_computation.4 | async-start | bytes 2097152 | tf_op jit(solution)/shard_map/all_to_all | solution.py:46
  61.5 21.5 %all-to-all-start.2 = ((bf16[32,4,2,2048]{3,2,1,0:T(2,128)(2,1)}), bf16[32,4,2,2048]{3,2,1,0:T(2,128)(2,1)}, u32[]{:S(2)}, u32[]{:S(2)}) async-start(bf16[32,4,2,2048]{3,2,1,0:T(2,128)(2,1)} %reshape.125), calls=%async_computation.2 | async-start | bytes 2097152 | tf_op jit(solution)/shard_map/all_to_all | solution.py:47
  85.8 52.6 %all-to-all-start.5 = ((bf16[32,8,2,2048]{3,2,0,1:T(2,128)(2,1)}), bf16[32,8,2,2048]{3,2,0,1:T(2,128)(2,1)}, u32[]{:S(2)}, u32[]{:S(2)}) async-start(bf16[32,8,2,2048]{3,2,0,1:T(2,128)(2,1)} %bitcast.63), calls=%async_computation.5 | async-start | bytes 4194304 | tf_op jit(solution)/shard_map/all_to_all | solution.py:51
  141.2 54.1 %all-to-all-start.3 = ((bf16[32,8,2,2048]{3,2,0,1:T(2,128)(2,1)}), bf16[32,8,2,2048]{3,2,0,1:T(2,128)(2,1)}, u32[]{:S(2)}, u32[]{:S(2)}) async-start(bf16[32,8,2,2048]{3,2,0,1:T(2,128)(2,1)} %bitcast.62), calls=%async_computation.3 | async-start | bytes 4194304 | tf_op jit(solution)/shard_map/all_to_all | solution.py:52
  146.4 58.3 %copy-start.9 = (f32[512]{0:T(512)}, f32[512]{0:T(512)S(1)}, u32[]{:S(2)}) copy-start(f32[512]{0:T(512)S(1)} %reshape.136) | copy-start | bytes 6148
  155.8 3.7 copy-start.2
  155.8 3.7 copy-start.5
  211.8 20.9 %all-to-all-start.8 = ((f32[32,8,2]{0,2,1:T(2,128)}), f32[32,8,2]{0,2,1:T(2,128)S(1)}, u32[]{:S(2)}, u32[]{:S(2)}) async-start(f32[32,8,2]{0,2,1:T(2,128)} %copy.103), calls=%async_computation.8 | async-start | bytes 16384 | tf_op jit(solution)/shard_map/all_to_all | solution.py:94
  215.4 1.3 copy-start.6
  232.7 98.8 %all-to-all-start.6 = ((f32[32,8,2,2048]{3,2,0,1:T(2,128)}), f32[32,8,2,2048]{3,2,0,1:T(2,128)}, u32[]{:S(2)}, u32[]{:S(2)}) async-start(f32[32,8,2,2048]{3,2,0,1:T(2,128)} %copy.100), calls=%async_computation.6 | async-start | bytes 8388608 | tf_op jit(solution)/shard_map/all_to_all | solution.py:93
  331.5 19.2 %all-to-all-start.9 = ((f32[32,8,2]{1,2,0:T(2,128)}), f32[32,8,2]{1,2,0:T(2,128)S(1)}, u32[]{:S(2)}, u32[]{:S(2)}) async-start(f32[32,8,2]{1,2,0:T(2,128)} %copy.104), calls=%async_computation.9 | async-start | bytes 65536 | tf_op jit(solution)/shard_map/all_to_all | solution.py:98
  350.7 59.3 %all-to-all-start.7 = ((f32[32,8,2,2048]{3,2,1,0:T(2,128)}), f32[32,8,2,2048]{3,2,1,0:T(2,128)}, u32[]{:S(2)}, u32[]{:S(2)}) async-start(f32[32,8,2,2048]{3,2,1,0:T(2,128)} %copy.101), calls=%async_computation.7 | async-start | bytes 8388608 | tf_op jit(solution)/shard_map/all_to_all | solution.py:97
  358.0 4.2 %copy-start.3 = (bf16[512,2048]{1,0:T(8,128)(2,1)S(1)}, bf16[512,2048]{1,0:T(8,128)(2,1)}, u32[]{:S(2)}) copy-start(bf16[512,2048]{1,0:T(8,128)(2,1)} %reshape.130) | copy-start | bytes 6291460
  358.0 4.2 %copy-start.7 = (bf16[512,384]{0,1:T(8,128)(2,1)S(1)}, bf16[512,384]{0,1:T(8,128)(2,1)}, u32[]{:S(2)}) copy-start(bf16[512,384]{0,1:T(8,128)(2,1)} %get-tuple-element.33) | copy-start | bytes 1179652
  362.2 2.5 copy-start.4
  362.2 2.5 copy-start.10
  362.3 2.5 copy-start.11
  410.0 4.7 %copy-start.1 = (bf16[1,2048,384]{2,1,0:T(8,128)(2,1)S(1)}, bf16[1,2048,384]{2,1,0:T(8,128)(2,1)}, u32[]{:S(2)}) copy-start(bf16[1,2048,384]{2,1,0:T(8,128)(2,1)} %param.11) | copy-start | bytes 4718596
where the time goes:
time: 417 us; the launch traced here: 415 us
  waiting for transfers between devices  249 us (60%)
  local copies, waits for them, and re-layouts  69 us (17%)
  starting transfers between devices  65.7 us (16%)
  matrix products  25.2 us (6%)
  other arithmetic  4.68 us (1%)
    all_to_all x1, waiting for transfers between devices, local(): lax.all_to_all(term_blocks, 'dp', split_axis=1, concat_axis=1, tiled=True)  91.8 us
    all_to_all x1, waiting for transfers between devices, local(): lax.all_to_all(doubled(by_column[0]), 'dp', split_axis=1, concat_axis=1,...  46.2 us
    all_to_all x1, waiting for transfers between devices, local(): lax.all_to_all(row_back[0], 'expert', split_axis=0, concat_axis=0, tiled=...  39.6 us
    all_to_all x1, waiting for transfers between devices, local(): lax.all_to_all(doubled(by_column[1]), 'dp', split_axis=1, concat_axis=1,...  34 us
    all_to_all x1, waiting for transfers between devices, local(): lax.all_to_all(send_grads, 'expert', split_axis=0, concat_axis=0, tiled=T...  15 us
    all_to_all x1, waiting for transfers between devices, local(): lax.all_to_all(send_rows, 'expert', split_axis=0, concat_axis=0, tiled=True)  14.2 us
    reshape x2, local copies, waits for them, and re-layouts, local(): term_blocks = half_term.reshape(recv_shape)  12.7 us
    all_to_all x1, starting transfers between devices, local(): lax.all_to_all(row_back[1], 'expert', split_axis=0, concat_axis=0, tiled=...  11.9 us
  transfers between devices with their start and end apart: 10, of which 9 were waited for; matrix products, arithmetic and copies ran while one was open for 16% of the time, Pallas kernels for 0%

commit v1 on v0

v1 whole, which is shorter than its diff:
```python
import jax
import jax.numpy as jnp
from jax import lax
from jax.sharding import PartitionSpec as P


def local(tokens, upstream, gate_probs, routes, w_gate, w_up, w_down):
    columns = lax.axis_size("expert")
    rows = lax.axis_size("dp")
    token_count, width = tokens.shape
    top = routes.shape[1]
    experts = columns * rows // 2
    reach = token_count * top // experts
    per_dest = rows * reach
    pair = lax.axis_index("dp") // 2
    f32, bf16 = jnp.float32, jnp.bfloat16

    hit = routes[:, :, None] == jnp.arange(experts, dtype=jnp.int32)[None, None, :]
    named = jnp.any(hit, axis=1)
    rank = jnp.cumsum(named.astype(jnp.int32), axis=0)
    key = jnp.where(named, rank, 0).astype(bf16)
    weight = jnp.sum(jnp.where(hit, gate_probs[:, :, None].astype(f32), 0.0), axis=1).astype(bf16)
    all_tokens = lax.all_gather(tokens, "dp", axis=0, tiled=True)
    all_upstream = lax.all_gather(upstream, "dp", axis=0, tiled=True)
    info = lax.all_gather(jnp.concatenate([key, weight], axis=1), "dp", axis=0, tiled=True)
    info = info.reshape(rows * token_count, 2, columns, rows // 2)
    info = lax.dynamic_index_in_dim(info, pair, axis=3, keepdims=False)
    key_all, weight_all = info[:, 0], info[:, 1]
    source = (jnp.arange(rows * token_count) // token_count).astype(jnp.int32)
    place = jnp.where(key_all > 0, key_all.astype(jnp.int32) - 1 + reach * source[:, None], -1)
    pick = place.T[:, None, :] == jnp.arange(per_dest, dtype=jnp.int32)[None, :, None]
    pick_scaled = jnp.where(pick, weight_all.T[:, None, :], 0).astype(bf16).reshape(columns * per_dest, -1)
    pick = pick.astype(bf16).reshape(columns * per_dest, -1)
    send_rows = jnp.dot(pick, all_tokens, preferred_element_type=f32).astype(bf16)
    send_scaled = jnp.dot(pick_scaled, all_upstream, preferred_element_type=f32).astype(bf16)
    x = lax.all_to_all(send_rows, "expert", split_axis=0, concat_axis=0, tiled=True)
    scaled = lax.all_to_all(send_scaled, "expert", split_axis=0, concat_axis=0, tiled=True)

    wg, wu, wd = w_gate[0], w_up[0], w_down[0]
    over_rows = (((0,), (0,)), ((), ()))
    over_cols = (((1,), (1,)), ((), ()))
    pre_gate = jnp.dot(x, wg, preferred_element_type=f32)
    pre_up = jnp.dot(x, wu, preferred_element_type=f32)
    sigmoid = jax.nn.sigmoid(pre_gate)
    activation = pre_gate * sigmoid
    derivative = sigmoid * (1.0 + pre_gate * (1.0 - sigmoid))
    hidden = (activation * pre_up).astype(bf16)
    back = lax.dot_general(scaled, wd, over_cols, preferred_element_type=f32)
    partial = jnp.sum(hidden.astype(f32) * back, axis=1)
    gate_delta = (back * pre_up * derivative).astype(bf16)
    up_delta = (back * activation).astype(bf16)
    half_term = lax.dot_general(gate_delta, wg, over_cols, preferred_element_type=f32) + lax.dot_general(
        up_delta, wu, over_cols, preferred_element_type=f32
    )
    own_expert = lax.axis_index("expert") * (rows // 2) + pair
    marked = jnp.where(jnp.arange(experts)[None, :] == own_expert, partial[:, None], 0.0)
    back_rows = jnp.concatenate([half_term.astype(bf16), marked.astype(bf16)], axis=1)
    returned = lax.all_to_all(back_rows, "expert", split_axis=0, concat_axis=0, tiled=True)
    summed = lax.dot_general(pick, returned, over_rows, preferred_element_type=f32)
    total = lax.psum_scatter(summed, "dp", scatter_dimension=0, tiled=True)
    input_grad = total[:, :width].astype(bf16)
    route_partial = jnp.sum(jnp.where(hit, total[:, None, width:], 0.0), axis=2) / gate_probs.astype(f32)
    gate_prob_grad = route_partial.astype(bf16).astype(f32)
    gate_weight_grad = lax.dot_general(x, gate_delta, over_rows, preferred_element_type=f32).astype(bf16)[None]
    up_weight_grad = lax.dot_general(x, up_delta, over_rows, preferred_element_type=f32).astype(bf16)[None]
    down_weight_grad = lax.dot_general(hidden, scaled, over_rows, preferred_element_type=f32).astype(bf16)[None]
    return input_grad, gate_prob_grad, gate_weight_grad, up_weight_grad, down_weight_grad


def solution(mesh):
    both = ("expert", "dp")
    flat, deep = P(both, None), P(both, None, None)
    return jax.shard_map(
        local,
        mesh=mesh,
        in_specs=(flat, flat, flat, flat, deep, deep, deep),
        out_specs=(flat, flat, deep, deep, deep),
        check_vma=False,
    )
```

time: 417 us -> 222 us (0.53)
  waiting for transfers between devices: 249 us -> 82.5 us
  local copies, waits for them, and re-layouts: 69 us -> 4.89 us
  blocking collectives: 0 us -> 57.1 us
  starting transfers between devices: 65.7 us -> 22.6 us
  between operations: 0.98 us -> 14 us
  matrix products: 25.2 us -> 35 us
    all_to_all x9 -> x1, waiting for transfers between devices: 235 us -> 20.7 us  [local(): lax.all_to_all(send_scaled, 'expert', split_axis=0, concat_axis=0, tiled=...]
    all_to_all x9 -> x1, starting transfers between devices: 59.4 us -> 10.7 us  [local(): lax.all_to_all(send_scaled, 'expert', split_axis=0, concat_axis=0, tiled=...]
    all_gather x0 -> x2, waiting for transfers between devices: none -> 38.3 us  [the longest x1 24.4 us: local(): all_upstream = lax.all_gather(upstream, 'dp', axis=0, tiled=True)]
    all_to_all x0 -> x1, blocking collectives: none -> 33.8 us  [local(): lax.all_to_all(back_rows, 'expert', split_axis=0, concat_axis=0, tiled=True)]
    reshape x13 -> x1, local copies, waits for them, and re-layouts: 27.7 us -> 0.04 us  [local(): info = info.reshape(rows * token_count, 2, columns, rows // 2)]
    all_gather x0 -> x1, blocking collectives: none -> 23.2 us  [local(): lax.all_gather(jnp.concatenate([key, weight], axis=1), 'dp', axis=0, tile...]
    all_to_all x8 -> x0, local copies, waits for them, and re-layouts: 22.2 us -> none  [the longest x1 6.92 us: local(): lax.all_to_all(term_blocks, 'dp', split_axis=1, concat_axis=1, tiled=True)]
    reduce_scatter x0 -> x1, waiting for transfers between devices: none -> 21.6 us  [local(): total = lax.psum_scatter(summed, 'dp', scatter_dimension=0, tiled=True)]
  transfers between devices with their start and end apart: 10 -> 5, of which waited for: 9 -> 5; matrix products, arithmetic and copies ran while one was open for 16% -> 13% of each run, Pallas kernels for 0% -> 0%
where the time goes in v1:
time: 222 us; the launch traced here: 218 us
  waiting for transfers between devices  82.5 us (37%)
  blocking collectives  57.1 us (26%)
  matrix products  35 us (16%)
  starting transfers between devices  22.6 us (10%)
  between operations  14 us (6%)
  local copies, waits for them, and re-layouts  4.89 us (2%)
    all_to_all x1, blocking collectives, local(): lax.all_to_all(back_rows, 'expert', split_axis=0, concat_axis=0, tiled=True)  33.8 us
    all_gather x1, waiting for transfers between devices, local(): all_upstream = lax.all_gather(upstream, 'dp', axis=0, tiled=True)  24.4 us
    all_gather x1, blocking collectives, local(): lax.all_gather(jnp.concatenate([key, weight], axis=1), 'dp', axis=0, tile...  23.2 us
    reduce_scatter x1, waiting for transfers between devices, local(): total = lax.psum_scatter(summed, 'dp', scatter_dimension=0, tiled=True)  21.6 us
    all_to_all x1, waiting for transfers between devices, local(): lax.all_to_all(send_scaled, 'expert', split_axis=0, concat_axis=0, tiled=...  20.7 us
    all_gather x1, waiting for transfers between devices, local(): all_tokens = lax.all_gather(tokens, 'dp', axis=0, tiled=True)  13.9 us
    all_to_all x1, starting transfers between devices, local(): lax.all_to_all(send_rows, 'expert', split_axis=0, concat_axis=0, tiled=True)  11.7 us
    all_to_all x1, starting transfers between devices, local(): lax.all_to_all(send_scaled, 'expert', split_axis=0, concat_axis=0, tiled=...  10.7 us
  transfers between devices with their start and end apart: 5, of which 5 were waited for; matrix products, arithmetic and copies ran while one was open for 13% of the time, Pallas kernels for 0%

profile of v1, /device:TPU:1, one launch (start us, length us, event | category | flops | bytes accessed | tf_op | source)
XLA Modules:
  0.0 217.7 jit_solution(13919623257304418479)
XLA Ops:
  7.2 0.0 copy-start
  7.2 0.0 all-gather.5.cloned.1.call-start
  7.2 0.7 all-gather.5.cloned.1.call-update
  7.9 0.0 all-gather.3.cloned.1.call-start
  8.0 0.7 all-gather.3.cloned.1.call-update
  8.7 0.8 copy.24
  9.5 0.0 copy-start.6
  9.5 0.8 copy.23
  10.2 0.1 fusion.14
  10.4 0.1 reduce_window_sum.11
  10.4 0.2 select_reduce_fusion.1
  10.6 0.1 eq.57
  10.7 0.0 copy-done.6
  10.7 23.2 %all_gather.9 = bf16[256,256]{1,0:T(8,128)(2,1)S(1)} all-gather(bf16[32,256]{1,0:T(8,128)(2,1)S(1)} %pad_maximum_fusion.1), channel_id=1, replica_groups=mesh['expert'=32,'dp'=8] {'dp'}, dimensions={0}, use_global_device_ids=true | all-gather | bytes 147456 | tf_op jit(solution)/shard_map/all_gather | solution.py:25
  33.9 0.1 copy.25
  34.1 0.1 constant_dynamic-slice_fusion
  34.2 0.0 copy-start.2
  34.2 0.1 bitcast_compare_fusion
  34.4 13.9 %all-gather.5.cloned.1.call-done = bf16[256,2048]{1,0:T(8,128)(2,1)} async-done(((bf16[32,2048]{1,0:T(8,128)(2,1)}), bf16[256,2048]{1,0:T(8,128)(2,1)}) %all-gather.5.cloned.1.call-update) | async-done | bytes 1048592 | tf_op jit(solution)/shard_map/all_gather | solution.py:23
  48.3 3.3 %convolution_convert_fusion = bf16[512,2048]{1,0:T(8,128)(2,1)} fusion(pred[512,256]{1,0:T(32,128)(4,1)S(1)} %bitcast_compare_fusion, bf16[256,2048]{1,0:T(8,128)(2,1)} %all-gather.5.cloned.1.call-done), kind=kOutput, calls=%fused_computation.2 | convolution fusion | flops 537919488 | bytes 3276800 | tf_op jit(solution)/shard_map/dot_general | solution.py:34
  51.6 11.7 %all-to-all-start.1 = ((bf16[32,16,2048]{2,1,0:T(8,128)(2,1)}), bf16[32,16,2048]{2,1,0:T(8,128)(2,1)}, u32[]{:S(2)}, u32[]{:S(2)}) async-start(bf16[32,16,2048]{2,1,0:T(8,128)(2,1)} %bitcast.71), calls=%async_computation.1 | async-start | bytes 4194304 | tf_op jit(solution)/shard_map/all_to_all | solution.py:36
  63.3 0.0 copy-done.2
  63.3 0.1 bitcast_select_fusion
  63.4 24.4 %all-gather.3.cloned.1.call-done = bf16[256,2048]{1,0:T(8,128)(2,1)} async-done(((bf16[32,2048]{1,0:T(8,128)(2,1)}), bf16[256,2048]{1,0:T(8,128)(2,1)}) %all-gather.3.cloned.1.call-update) | async-done | bytes 1048592 | tf_op jit(solution)/shard_map/all_gather | solution.py:24
  87.8 3.3 %convolution_convert_fusion.1 = bf16[512,2048]{1,0:T(8,128)(2,1)} fusion(bf16[512,256]{1,0:T(8,128)(2,1)S(1)} %bitcast_select_fusion, bf16[256,2048]{1,0:T(8,128)(2,1)} %all-gather.3.cloned.1.call-done), kind=kOutput, calls=%fused_computation.3 | convolution fusion | flops 537919488 | bytes 3407872 | tf_op jit(solution)/shard_map/dot_general | solution.py:35
  91.1 0.5 all-to-all-done.1
  91.6 10.7 %all-to-all-start = ((bf16[32,16,2048]{2,1,0:T(8,128)(2,1)}), bf16[32,16,2048]{2,1,0:T(8,128)(2,1)}, u32[]{:S(2)}, u32[]{:S(2)}) async-start(bf16[32,16,2048]{2,1,0:T(8,128)(2,1)} %bitcast.70), calls=%async_computation | async-start | bytes 4194304 | tf_op jit(solution)/shard_map/all_to_all | solution.py:37
  102.4 0.0 reduce-scatter.2.cloned.1.call-start
  102.4 0.5 iota_compare_fusion.3
  102.9 0.0 copy-done
  102.9 0.0 copy-start.1
  102.9 3.6 %fusion.5 = f32[512,384]{0,1:T(8,128)} fusion(bf16[512,2048]{1,0:T(8,128)(2,1)} %bitcast.11, bf16[1,2048,384]{2,1,0:T(8,128)(2,1)S(1)} %copy-done), kind=kOutput, calls=%fused_computation.13 | convolution fusion | flops 805306368 | bytes 4456448 | tf_op jit(solution)/shard_map/dot_general | solution.py:42
  106.6 0.0 copy-done.1
  106.6 3.5 %fusion.8 = f32[512,384]{0,1:T(8,128)} fusion(bf16[512,2048]{1,0:T(8,128)(2,1)} %bitcast.11, bf16[1,2048,384]{2,1,0:T(8,128)(2,1)S(1)} %copy-done.1), kind=kOutput, calls=%fused_computation.16 | convolution fusion | flops 805306368 | bytes 4456448 | tf_op jit(solution)/shard_map/dot_general | solution.py:43
  110.0 20.7 %all-to-all-done = bf16[32,16,2048]{2,1,0:T(8,128)(2,1)} async-done(((bf16[32,16,2048]{2,1,0:T(8,128)(2,1)}), bf16[32,16,2048]{2,1,0:T(8,128)(2,1)}, u32[]{:S(2)}, u32[]{:S(2)}) %all-to-all-start) | async-done | bytes 2097184 | tf_op jit(solution)/shard_map/all_to_all | solution.py:37
  130.7 4.6 %multiply_reduce_fusion = (bf16[512]{0:T(512)(128)(2,1)S(1)}, bf16[512,384]{0,1:T(8,128)(2,1)}, bf16[512,384]{0,1:T(8,128)(2,1)S(1)}, bf16[512,384]{0,1:T(8,128)(2,1)S(1)}) fusion(f32[512,384]{0,1:T(8,128)} %fusion.8, f32[512,384]{0,1:T(8,128)} %fusion.5, bf16[512,2048]{1,0:T(8,128)(2,1)} %bitcast.8, bf16[1,384,2048]{2,1,0:T(8,128)(2,1)} %param.13), kind=kOutput, calls=%fused_computation.20 | convolution fusion | flops 808844800 | bytes 6423552 | tf_op jit(solution)/shard_map/dot_general | solution.py:48
  135.3 0.0 copy-start.4
  135.3 0.0 copy-start.8
  135.3 1.3 fusion.3
  136.6 0.0 copy-done.8
  136.6 0.1 select_convert_fusion
  136.7 0.0 copy-done.4
  136.7 1.3 add_convert_fusion
  138.1 0.2 pad_maximum_fusion
  138.3 0.0 copy-start.3
  138.3 33.8 %all_to_all.33 = bf16[32,16,2176]{2,1,0:T(8,128)(2,1)S(1)} all-to-all(bf16[32,16,2176]{2,1,0:T(8,128)(2,1)S(1)} %bitcast.69), channel_id=1, replica_groups=mesh['expert'=32,'dp'=8] {'expert'}, dimensions={0} | all-to-all | bytes 4456448 | tf_op jit(solution)/shard_map/all_to_all | solution.py:58
  172.1 0.0 copy-done.3
  172.1 2.2 %convolution_bitcast_fusion = f32[256,2176]{1,0:T(8,128)} fusion(bf16[32,16,2176]{2,1,0:T(8,128)(2,1)S(1)} %all_to_all.33, s32[32,256]{1,0:T(8,128)S(1)} %copy-done.3), kind=kOutput, calls=%fused_computation.1 | convolution fusion | flops 570556416 | bytes 4489216 | tf_op jit(solution)/shard_map/dot_general | solution.py:59
  174.3 0.0 reduce-scatter.2.cloned.1.call-update
  174.4 0.0 copy-start.5
  174.4 4.1 %fusion = bf16[1,2048,384]{2,1,0:T(8,128)(2,1)} fusion(bf16[512,2048]{1,0:T(8,128)(2,1)} %bitcast.11, bf16[512,384]{0,1:T(8,128)(2,1)S(1)} %get-tuple-element.12), kind=kOutput, calls=%fused_computation.7 | convolution fusion | flops 806092800 | bytes 4063232 | tf_op jit(solution)/shard_map/dot_general | solution.py:64
  178.5 0.0 copy-done.5
  178.5 0.0 copy-start.9
  178.5 4.1 %fusion.1 = bf16[1,2048,384]{2,1,0:T(8,128)(2,1)} fusion(bf16[512,2048]{1,0:T(8,128)(2,1)} %bitcast.11, bf16[512,384]{0,1:T(8,128)(2,1)S(1)} %copy-done.5), kind=kOutput, calls=%fused_computation.8 | convolution fusion | flops 806092800 | bytes 4063232 | tf_op jit(solution)/shard_map/dot_general | solution.py:65
  182.6 0.0 copy-done.9
  182.6 0.0 copy-start.7
  182.6 3.7 %fusion.2 = bf16[1,384,2048]{2,1,0:T(8,128)(2,1)} fusion(bf16[512,384]{0,1:T(8,128)(2,1)S(1)} %copy-done.9, bf16[512,2048]{1,0:T(8,128)(2,1)} %bitcast.8), kind=kOutput, calls=%fused_computation.9 | convolution fusion | flops 806092800 | bytes 4063232 | tf_op jit(solution)/shard_map/dot_general | solution.py:66
  186.3 21.6 %reduce-scatter.2.cloned.1.call-done = f32[32,2176]{1,0:T(8,128)} async-done(((f32[256,2176]{1,0:T(8,128)}), f32[32,2176]{1,0:T(8,128)}) %reduce-scatter.2.cloned.1.call-update) | async-done | bytes 278544 | tf_op jit(solution)/shard_map/reduce_scatter | solution.py:60
  207.9 0.7 slice.20
  208.7 0.2 select_reduce_fusion
  208.8 0.0 copy-done.7
  208.9 0.7 copy.26
  209.5 1.6 slice.24
  (11 shorter events, 0.1 us)
Async XLA Ops:
  7.2 95.8 %copy-start = (bf16[1,2048,384]{2,1,0:T(8,128)(2,1)S(1)}, bf16[1,2048,384]{2,1,0:T(8,128)(2,1)}, u32[]{:S(2)}) copy-start(bf16[1,2048,384]{2,1,0:T(8,128)(2,1)} %param.11) | copy-start | bytes 4718596
  7.2 41.1 %all-gather.5.cloned.1.call-start = ((), (), s32[]{:S(2)}) async-start(), calls=%async_computation.5 | async-start | bytes 1179648 | tf_op jit(solution)/shard_map/all_gather | solution.py:23
  7.9 79.9 %all-gather.3.cloned.1.call-start = ((), (), s32[]{:S(2)}) async-start(), calls=%async_computation.4 | async-start | bytes 1179648 | tf_op jit(solution)/shard_map/all_gather | solution.py:24
  9.5 1.2 copy-start.6
  34.2 29.1 %copy-start.2 = (s32[32,256]{1,0:T(8,128)}, s32[32,256]{1,0:T(8,128)S(1)}, u32[]{:S(2)}) copy-start(s32[32,256]{1,0:T(8,128)S(1)} %fusion.16) | copy-start | bytes 98308
  51.6 40.0 %all-to-all-start.1 = ((bf16[32,16,2048]{2,1,0:T(8,128)(2,1)}), bf16[32,16,2048]{2,1,0:T(8,128)(2,1)}, u32[]{:S(2)}, u32[]{:S(2)}) async-start(bf16[32,16,2048]{2,1,0:T(8,128)(2,1)} %bitcast.71), calls=%async_computation.1 | async-start | bytes 4194304 | tf_op jit(solution)/shard_map/all_to_all | solution.py:36
  91.6 39.1 %all-to-all-start = ((bf16[32,16,2048]{2,1,0:T(8,128)(2,1)}), bf16[32,16,2048]{2,1,0:T(8,128)(2,1)}, u32[]{:S(2)}, u32[]{:S(2)}) async-start(bf16[32,16,2048]{2,1,0:T(8,128)(2,1)} %bitcast.70), calls=%async_computation | async-start | bytes 4194304 | tf_op jit(solution)/shard_map/all_to_all | solution.py:37
  102.4 105.6 %reduce-scatter.2.cloned.1.call-start = ((), (), s32[]{:S(2)}) async-start(), calls=%async_computation.6 | async-start | bytes 2506752 | tf_op jit(solution)/shard_map/reduce_scatter | solution.py:60
  102.9 3.6 %copy-start.1 = (bf16[1,2048,384]{2,1,0:T(8,128)(2,1)S(1)}, bf16[1,2048,384]{2,1,0:T(8,128)(2,1)}, u32[]{:S(2)}) copy-start(bf16[1,2048,384]{2,1,0:T(8,128)(2,1)} %param.12) | copy-start | bytes 4718596
  135.3 1.5 copy-start.4
  135.3 1.3 copy-start.8
  138.3 33.8 %copy-start.3 = (s32[32,256]{1,0:T(8,128)S(1)}, s32[32,256]{1,0:T(8,128)}, u32[]{:S(2)}) copy-start(s32[32,256]{1,0:T(8,128)} %copy-done.2) | copy-start | bytes 98308
  174.4 4.1 %copy-start.5 = (bf16[512,384]{0,1:T(8,128)(2,1)S(1)}, bf16[512,384]{0,1:T(8,128)(2,1)}, u32[]{:S(2)}) copy-start(bf16[512,384]{0,1:T(8,128)(2,1)} %copy-done.4) | copy-start | bytes 1179652
  178.5 4.1 %copy-start.9 = (bf16[512,384]{0,1:T(8,128)(2,1)S(1)}, bf16[512,384]{0,1:T(8,128)(2,1)}, u32[]{:S(2)}) copy-start(bf16[512,384]{0,1:T(8,128)(2,1)} %get-tuple-element.11) | copy-start | bytes 1179652
  182.6 26.3 %copy-start.7 = (bf16[32,8]{1,0:T(8,128)(2,1)S(1)}, bf16[32,8]{1,0:T(8,128)(2,1)}, u32[]{:S(2)}) copy-start(bf16[32,8]{1,0:T(8,128)(2,1)} %copy-done.6) | copy-start | bytes 1540
Sparse Core Ops, SparseCore 0:
  9.8 38.4 all-gather.4
  50.1 37.7 all-gather.2
  174.5 33.4 reduce-scatter.1

commit v2 on v1

v2 whole, which is shorter than its diff:
```python
import functools
import math

import jax
import jax.numpy as jnp
from jax import lax
from jax.experimental import pallas as pl
from jax.experimental.pallas import tpu as pltpu
from jax.sharding import PartitionSpec as P

MESH = pl.DeviceIdType.MESH
F32, BF16 = jnp.float32, jnp.bfloat16
NT = (((1,), (1,)), ((), ()))
TN = (((0,), (0,)), ((), ()))


def dot(a, b, dims=(((1,), (0,)), ((), ()))):
    return lax.dot_general(a, b, dims, preferred_element_type=F32)


def tiles(count, body):
    def step(i, carry):
        body(i)
        return carry

    lax.fori_loop(0, count, step, 0)


def kernel(sizes, *refs):
    columns, rows, tokens, width, experts, units, top, halves, returns = sizes
    (tok_hbm, ups_hbm, probs, routes, wg_hbm, wu_hbm, wd_hbm, input_grad, prob_grad, gate_out, up_out, down_out) = refs[:12]
    (ring, info, pick, pick_scaled, merge, send, recv, wgu, wd, acc, acc_back, hidden, delta, grad_gu, grad_d) = refs[12:27]
    refs = refs[27:]
    back_send, back_recv = refs[:returns], refs[returns : 2 * returns]
    row_send, row_recv = refs[2 * returns : 3 * returns], refs[3 * returns : 4 * returns]
    (own_sem, weight_sem, out_sem, ring_send_sem, ring_recv_sem, info_send_sem, info_recv_sem) = refs[4 * returns : 4 * returns + 7]
    (send_sem, recv_sem, back_send_sem, back_recv_sem, row_send_sem, row_recv_sem) = refs[4 * returns + 7 :]

    reach = tokens * top // experts
    per_dest = rows * reach
    slots = columns * per_dest
    waves = 2 * halves
    chunk = width // halves
    part = width // returns
    side = math.isqrt(columns // 2)
    me_c, me_r = lax.axis_index("expert"), lax.axis_index("dp")
    core, me_y, me_x = lax.rem(me_c, 2), lax.rem(me_c // 2, side), me_c // (2 * side)
    pair = me_r // 2

    def row_at(offset):
        return lax.rem(me_r + (offset % rows), rows)

    def column_at(i):
        dc, dy, dx = lax.rem(i, 2), lax.rem(i // 2, side), i // (2 * side)
        x, y = lax.rem(me_x + dx, side), lax.rem(me_y + dy, side)
        return (x * side + y) * 2 + lax.rem(core + dc, 2)

    def mixed(i):
        return lax.rem(i * 11, columns)

    own_copies = []
    for w in range(waves):
        source = (tok_hbm, ups_hbm)[w // halves].at[:, pl.ds((w % halves) * chunk, chunk)]
        copy = pltpu.make_async_copy(source, ring.at[w, me_r], own_sem.at[w])
        copy.start()
        own_copies.append(copy)
    weight_copies = [
        pltpu.make_async_copy(wg_hbm.at[0], wgu.at[:, pl.ds(0, units)], weight_sem.at[0]),
        pltpu.make_async_copy(wu_hbm.at[0], wgu.at[:, pl.ds(units, units)], weight_sem.at[1]),
        pltpu.make_async_copy(wd_hbm.at[0], wd, weight_sem.at[2]),
    ]
    for copy in weight_copies:
        copy.start()

    barrier = pltpu.get_barrier_semaphore()

    def greet_column(i):
        pl.semaphore_signal(barrier, inc=1, device_id=(column_at(i + 1), me_r), device_id_type=MESH)

    tiles(columns - 1, greet_column)
    for offset in range(1, rows):
        pl.semaphore_signal(barrier, inc=1, device_id=(me_c, row_at(offset)), device_id_type=MESH)

    lane = lax.broadcasted_iota(jnp.int32, (tokens, experts), 1)
    named = jnp.zeros((tokens, experts), F32)
    weight = jnp.zeros((tokens, experts), F32)
    for k in range(top):
        hit = routes[:, k : k + 1] == lane
        named = jnp.where(hit, 1.0, named)
        weight = jnp.where(hit, probs[:, k : k + 1].astype(F32), weight)
    upto = lax.broadcasted_iota(jnp.int32, (tokens, tokens), 0) >= lax.broadcasted_iota(jnp.int32, (tokens, tokens), 1)
    upto = jnp.where(upto, 1.0, 0.0).astype(BF16)
    rank = named * dot(upto, named.astype(BF16))
    info[me_r, 0:tokens, :] = rank.astype(BF16)
    info[me_r, tokens : 2 * tokens, :] = weight.astype(BF16)

    pl.semaphore_wait(barrier, columns - 1 + rows - 1)

    info_copies = []
    for offset in range(1, rows):
        copy = pltpu.make_async_remote_copy(
            info.at[me_r], info.at[me_r], info_send_sem.at[offset], info_recv_sem.at[offset],
            device_id=(me_c, row_at(offset)), device_id_type=MESH,
        )
        copy.start()
        info_copies.append(copy)

    reaches = (rows // 2, rows - 1 - rows // 2)

    def ring_copy(w, d, step):
        sign = (1 if w % 2 == 0 else -1) * (1 if d == 0 else -1)
        source = row_at(-sign * step)
        return pltpu.make_async_remote_copy(
            ring.at[w, source], ring.at[w, source], ring_send_sem.at[w, d, step], ring_recv_sem.at[w, d, step],
            device_id=(me_c, row_at(sign)), device_id_type=MESH,
        )

    def ring_arrived(w, d, step):
        sign = (1 if w % 2 == 0 else -1) * (1 if d == 0 else -1)
        source = row_at(-sign * (step + 1))
        pltpu.make_async_remote_copy(
            ring.at[w, source], ring.at[w, source], ring_send_sem.at[w, d, step], ring_recv_sem.at[w, d, step],
            device_id=(me_c, row_at(sign)), device_id_type=MESH,
        ).wait_recv()

    def make_picks():
        for offset in range(1, rows):
            source = row_at(-offset)
            pltpu.make_async_remote_copy(
                info.at[source], info.at[source], info_send_sem.at[offset], info_recv_sem.at[offset],
                device_id=(me_c, row_at(offset)), device_id_type=MESH,
            ).wait_recv()
        count = rows * tokens
        expert = lax.broadcasted_iota(jnp.int32, (experts, slots), 0)
        slot = lax.broadcasted_iota(jnp.int32, (experts, slots), 1)
        spread = jnp.where(expert == (slot // per_dest) * (rows // 2) + pair, 1.0, 0.0).astype(BF16)
        ranks = dot(info[:, 0:tokens, :].reshape(count, experts), spread)
        weights = dot(info[:, tokens : 2 * tokens, :].reshape(count, experts), spread)
        token = lax.broadcasted_iota(jnp.int32, (count, slots), 0)
        place = lax.broadcasted_iota(jnp.int32, (count, slots), 1)
        wanted = (lax.rem(place, per_dest) - reach * (token // tokens) + 1).astype(F32)
        match = (ranks > 0.5) & (ranks == wanted)
        ones = jnp.where(match, 1.0, 0.0)
        merge[...] = ones.astype(BF16)
        pick[...] = ones.T.astype(BF16)
        pick_scaled[...] = jnp.where(match, weights, 0.0).T.astype(BF16)

    step_columns = 256 if chunk % 256 == 0 else 128

    def send_wave(w):
        chosen = pick if w < halves else pick_scaled

        def one(i):
            at = pl.ds(pl.multiple_of(i * step_columns, step_columns), step_columns)
            block = ring[w, :, :, at].reshape(rows * tokens, step_columns)
            send[w, :, at] = dot(chosen[...], block).astype(BF16)

        tiles(chunk // step_columns, one)
        own = pl.ds(pl.multiple_of(me_c * per_dest, per_dest), per_dest)
        recv[w, own, :] = send[w, own, :]

        def ship(i):
            to = column_at(mixed(i + 1))
            pltpu.make_async_remote_copy(
                send.at[w, pl.ds(pl.multiple_of(to * per_dest, per_dest), per_dest)], recv.at[w, own],
                send_sem.at[w], recv_sem.at[w], device_id=(to, me_r), device_id_type=MESH,
            ).start()

        tiles(columns - 1, ship)

    for tick in range(waves + rows // 2):
        for w in range(waves):
            step = tick - w
            if step == 0:
                own_copies[w].wait()
            for d in range(2):
                if 1 <= step <= reaches[d]:
                    ring_arrived(w, d, step - 1)
                if 0 <= step < reaches[d]:
                    ring_copy(w, d, step).start()
        w = tick - rows // 2
        if w == 0:
            make_picks()
        if w >= 0:
            send_wave(w)

    for copy in weight_copies:
        copy.wait()

    others = (columns - 1) * per_dest

    def arrived(buffer, sem):
        pltpu.make_async_copy(buffer, buffer, sem).wait()

    unit_tile = 256 if (2 * units) % 256 == 0 else 128
    back_tile = 128
    for w in range(halves):
        arrived(recv.at[w, pl.ds(0, others)], recv_sem.at[w])

        def forward(i):
            at = pl.ds(pl.multiple_of(i * unit_tile, unit_tile), unit_tile)
            value = dot(recv[w], wgu[w * chunk : (w + 1) * chunk, at])
            acc[:, at] = value if w == 0 else acc[:, at] + value

        tiles(2 * units // unit_tile, forward)

    block_rows = 64

    def activate(i):
        at = pl.ds(pl.multiple_of(i * block_rows, block_rows), block_rows)
        gate, up = acc[at, 0:units], acc[at, units : 2 * units]
        sigmoid = jax.nn.sigmoid(gate)
        activation = gate * sigmoid
        hidden[at, :] = (activation * up).astype(BF16)
        acc[at, 0:units] = up * (sigmoid * (1.0 + gate * (1.0 - sigmoid)))
        acc[at, units : 2 * units] = activation

    tiles(slots // block_rows, activate)

    for w in range(halves, waves):
        arrived(recv.at[w, pl.ds(0, others)], recv_sem.at[w])
        start = (w - halves) * chunk

        def backward(i):
            at = pl.ds(pl.multiple_of(i * back_tile, back_tile), back_tile)
            value = dot(recv[w], wd[at, start : start + chunk], NT)
            acc_back[:, at] = value if w == halves else acc_back[:, at] + value

        tiles(units // back_tile, backward)

    own_expert = me_c * (rows // 2) + pair

    def deltas(i):
        at = pl.ds(pl.multiple_of(i * block_rows, block_rows), block_rows)
        back = acc_back[at, :]
        delta[at, 0:units] = (back * acc[at, 0:units]).astype(BF16)
        delta[at, units : 2 * units] = (back * acc[at, units : 2 * units]).astype(BF16)
        partial = jnp.sum(hidden[at, :].astype(F32) * back, axis=1, keepdims=True)
        place = lax.broadcasted_iota(jnp.int32, (block_rows, experts), 1)
        back_send[0][at, part : part + experts] = jnp.where(place == own_expert, partial, 0.0).astype(BF16)

    tiles(slots // block_rows, deltas)

    part_tile = 256 if part % 256 == 0 else 128
    own = pl.ds(pl.multiple_of(me_c * per_dest, per_dest), per_dest)
    for v in range(returns):

        def term(i):
            at = pl.ds(pl.multiple_of(i * part_tile, part_tile), part_tile)
            from_row = pl.ds(pl.multiple_of(v * part + i * part_tile, part_tile), part_tile)
            back_send[v][:, at] = dot(delta[...], wgu[from_row, :], NT).astype(BF16)

        tiles(part // part_tile, term)
        back_recv[v][own, :] = back_send[v][own, :]

        def ship_back(i):
            to = column_at(mixed(i + 1))
            pltpu.make_async_remote_copy(
                back_send[v].at[pl.ds(pl.multiple_of(to * per_dest, per_dest), per_dest)], back_recv[v].at[own],
                back_send_sem.at[v], back_recv_sem.at[v], device_id=(to, me_r), device_id_type=MESH,
            ).start()

        tiles(columns - 1, ship_back)

    out_copies = []
    grad_tile = 256 if chunk % 256 == 0 else 128

    def weight_gradients(w):
        def gate_up(i):
            at = pl.ds(pl.multiple_of(i * grad_tile, grad_tile), grad_tile)
            to = pl.ds(pl.multiple_of(w * chunk + i * grad_tile, grad_tile), grad_tile)
            grad_gu[to, :] = dot(recv[w, :, at], delta[...], TN).astype(BF16)

        def down(i):
            at = pl.ds(pl.multiple_of(i * grad_tile, grad_tile), grad_tile)
            to = pl.ds(pl.multiple_of(w * chunk + i * grad_tile, grad_tile), grad_tile)
            grad_d[:, to] = dot(hidden[...], recv[halves + w, :, at], TN).astype(BF16)

        tiles(chunk // grad_tile, gate_up)
        at = pl.ds(w * chunk, chunk)
        for n, out in enumerate((gate_out, up_out)):
            copy = pltpu.make_async_copy(grad_gu.at[at, pl.ds(n * units, units)], out.at[0, at, :], out_sem.at[n, w])
            copy.start()
            out_copies.append(copy)
        tiles(chunk // grad_tile, down)
        copy = pltpu.make_async_copy(grad_d.at[:, at], down_out.at[0, :, at], out_sem.at[2, w])
        copy.start()
        out_copies.append(copy)

    def combine(v):
        arrived(back_recv[v].at[pl.ds(0, others)], back_recv_sem.at[v])
        summed = dot(merge[...], back_recv[v][...]).astype(BF16).reshape(row_send[v].shape)
        row_send[v][...] = summed
        row_recv[v][me_r] = row_send[v][me_r]
        for offset in range(1, rows):
            to = row_at(offset)
            pltpu.make_async_remote_copy(
                row_send[v].at[to], row_recv[v].at[me_r], row_send_sem.at[v], row_recv_sem.at[v],
                device_id=(me_c, to), device_id_type=MESH,
            ).start()

    done = 0
    for v in range(returns):
        while done < halves and done * returns <= v * halves:
            weight_gradients(done)
            done = done + 1
        combine(v)

    for v in range(returns):
        arrived(row_recv[v].at[pl.ds(0, rows - 1)], row_recv_sem.at[v])
        total = row_recv[v][0].astype(F32)
        for r in range(1, rows):
            total = total + row_recv[v][r].astype(F32)
        input_grad[:, v * part : (v + 1) * part] = total[:, 0:part].astype(BF16)
        if v == 0:
            partials = total[:, part : part + experts]
            place = lax.broadcasted_iota(jnp.int32, (tokens, top), 1)
            result = jnp.zeros((tokens, top), F32)
            for k in range(top):
                own_value = jnp.sum(jnp.where(routes[:, k : k + 1] == lane, partials, 0.0), axis=1, keepdims=True)
                result = jnp.where(place == k, own_value, result)
            prob_grad[...] = (result / probs[...].astype(F32)).astype(BF16).astype(F32)

    for copy in info_copies:
        copy.wait_send()
    for w in range(waves):
        for d in range(2):
            for step in range(reaches[d]):
                ring_copy(w, d, step).wait_send()
        arrived(send.at[w, pl.ds(0, others)], send_sem.at[w])
    for v in range(returns):
        arrived(back_send[v].at[pl.ds(0, others)], back_send_sem.at[v])
        arrived(row_send[v].at[pl.ds(0, rows - 1)], row_send_sem.at[v])
    for copy in out_copies:
        copy.wait()


def local(halves, returns, tokens, upstream, gate_probs, routes, w_gate, w_up, w_down):
    columns, rows = lax.axis_size("expert"), lax.axis_size("dp")
    count, width = tokens.shape
    top = routes.shape[1]
    units = w_gate.shape[2]
    experts = columns * rows // 2
    per_dest = rows * (count * top // experts)
    slots = columns * per_dest
    waves, chunk, part = 2 * halves, width // halves, width // returns
    extra = [experts] + [0] * (returns - 1)
    dma = pltpu.SemaphoreType.DMA
    any_space, vmem = pl.BlockSpec(memory_space=pl.ANY), pl.BlockSpec(memory_space=pltpu.VMEM)
    return pl.pallas_call(
        functools.partial(kernel, (columns, rows, count, width, experts, units, top, halves, returns)),
        out_shape=[
            jax.ShapeDtypeStruct((count, width), BF16),
            jax.ShapeDtypeStruct((count, top), F32),
            jax.ShapeDtypeStruct(w_gate.shape, BF16),
            jax.ShapeDtypeStruct(w_up.shape, BF16),
            jax.ShapeDtypeStruct(w_down.shape, BF16),
        ],
        in_specs=[any_space, any_space, vmem, vmem, any_space, any_space, any_space],
        out_specs=[vmem, vmem, any_space, any_space, any_space],
        scratch_shapes=[
            pltpu.VMEM((waves, rows, count, chunk), BF16),
            pltpu.VMEM((rows, 2 * count, experts), BF16),
            pltpu.VMEM((slots, rows * count), BF16),
            pltpu.VMEM((slots, rows * count), BF16),
            pltpu.VMEM((rows * count, slots), BF16),
            pltpu.VMEM((waves, slots, chunk), BF16),
            pltpu.VMEM((waves, slots, chunk), BF16),
            pltpu.VMEM((width, 2 * units), BF16),
            pltpu.VMEM((units, width), BF16),
            pltpu.VMEM((slots, 2 * units), F32),
            pltpu.VMEM((slots, units), F32),
            pltpu.VMEM((slots, units), BF16),
            pltpu.VMEM((slots, 2 * units), BF16),
            pltpu.VMEM((width, 2 * units), BF16),
            pltpu.VMEM((units, width), BF16),
        ]
        + [pltpu.VMEM((slots, part + more), BF16) for more in extra] * 2
        + [pltpu.VMEM((rows, count, part + more), BF16) for more in extra] * 2
        + [
            dma((waves,)),
            dma((3,)),
            dma((3, halves)),
            dma((waves, 2, rows // 2)),
            dma((waves, 2, rows // 2)),
            dma((rows,)),
            dma((rows,)),
            dma((waves,)),
            dma((waves,)),
            dma((returns,)),
            dma((returns,)),
            dma((returns,)),
            dma((returns,)),
        ],
        compiler_params=pltpu.CompilerParams(
            collective_id=0, has_side_effects=True, vmem_limit_bytes=60 * 1024 * 1024
        ),
        cost_estimate=pl.CostEstimate(
            flops=16 * slots * width * units, bytes_accessed=24 * width * units, transcendentals=slots * units
        ),
    )(tokens, upstream, gate_probs, routes, w_gate, w_up, w_down)


def solution(mesh, halves=2, returns=4):
    both = ("expert", "dp")
    flat, deep = P(both, None), P(both, None, None)
    return jax.shard_map(
        functools.partial(local, halves, returns),
        mesh=mesh,
        in_specs=(flat, flat, flat, flat, deep, deep, deep),
        out_specs=(flat, flat, deep, deep, deep),
        check_vma=False,
    )
```

time: 222 us -> 137 us (0.62); the launches traced: 218 us -> 136 us
  Pallas kernels: 0 us -> 124 us
  waiting for transfers between devices: 82.5 us -> 0 us
  blocking collectives: 57.1 us -> 0 us
  matrix products: 35 us -> 0 us
  starting transfers between devices: 22.6 us -> 0 us
  between operations: 14 us -> 0.64 us
  local copies, waits for them, and re-layouts: 4.89 us -> 11.6 us
    pallas_call x0 -> x1, Pallas kernels: none -> 124 us  [local(): pl.pallas_call(functools.partial(kernel, (columns, rows, count, width, ex...]
    all_gather x2 -> x0, waiting for transfers between devices: 38.3 us -> none  [the longest x1 24.4 us: local(): all_upstream = lax.all_gather(upstream, 'dp', axis=0, tiled=True)]
    dot_general x11 -> x0, matrix products: 35 us -> none  [the longest x1 4.55 us: local(): back = lax.dot_general(scaled, wd, over_cols, preferred_element_type=f32)]
    all_to_all x1 -> x0, blocking collectives: 33.8 us -> none  [local(): lax.all_to_all(back_rows, 'expert', split_axis=0, concat_axis=0, tiled=True)]
    all_gather x1 -> x0, blocking collectives: 23.2 us -> none  [local(): lax.all_gather(jnp.concatenate([key, weight], axis=1), 'dp', axis=0, tile...]
    all_to_all x2 -> x0, starting transfers between devices: 22.4 us -> none  [the longest x1 11.7 us: local(): lax.all_to_all(send_rows, 'expert', split_axis=0, concat_axis=0, tiled=True)]
    reduce_scatter x1 -> x0, waiting for transfers between devices: 21.6 us -> none  [local(): total = lax.psum_scatter(summed, 'dp', scatter_dimension=0, tiled=True)]
    all_to_all x2 -> x0, waiting for transfers between devices: 21.1 us -> none  [the longest x1 20.7 us: local(): lax.all_to_all(send_scaled, 'expert', split_axis=0, concat_axis=0, tiled=...]
  transfers between devices with their start and end apart: 5 -> 0, of which waited for: 5 -> 0; matrix products, arithmetic and copies ran while one was open for 13% -> 0% of each run, Pallas kernels for 0% -> 0%
where the time goes in v2:
time: 137 us; the launch traced here: 136 us
  Pallas kernels  124 us (91%)
  local copies, waits for them, and re-layouts  11.6 us (8%)
    pallas_call x1, Pallas kernels, local(): pl.pallas_call(functools.partial(kernel, (columns, rows, count, width, ex...  124 us
    unnamed x10, local copies, waits for them, and re-layouts  10.2 us

profile of v2, /device:TPU:1, one launch (start us, length us, event | category | flops | bytes accessed | tf_op | source)
XLA Modules:
  0.0 136.3 jit_solution(5562209496407438197)
XLA Ops:
  0.6 1.4 copy.12.refs_2_
  2.0 1.4 %copy.13.refs_3_ = s32[32,8]{1,0:T(8,128)} copy(s32[32,8]{0,1:T(8,128)} %param.10) | data formatting | bytes 2048 | tf_op args[3]
  3.4 124.0 %shard_map.110 = (bf16[32,2048]{1,0:T(8,128)(2,1)}, f32[32,8]{1,0:T(8,128)}, bf16[1,2048,384]{2,1,0:T(8,128)(2,1)}, bf16[1,2048,384]{2,1,0:T(8,128)(2,1)}, bf16[1,384,2048]{2,1,0:T(8,128)(2,1)}) custom-call(bf16[32,2048]{1,0:T(8,128)(2,1)} %refs_0_.1, bf16[32,2048]{1,0:T(8,128)(2,1)} %refs_1_.1, bf16[32,8]{1,0:T(8,128)(2,1)} %copy.12.refs_2_, ...), custom_call_target="tpu_custom_call" | custom-call | flops 6442450944 | bytes 18874368 | tf_op jit(solution)/shard_map/pallas_call | solution.py:350
  127.4 1.4 %copy.14 = f32[32,8]{0,1:T(8,128)} copy(f32[32,8]{1,0:T(8,128)} %get-tuple-element.6) | data formatting | bytes 2048 | tf_op jit(solution)/shard_map/pallas_call | solution.py:350
  128.7 1.6 %copy.19 = bf16[32,2048]{1,0:T(8,128)(2,1)} copy(bf16[32,2048]{1,0:T(8,128)(2,1)} %get-tuple-element.15) | data formatting | bytes 262144
  130.3 0.0 copy-start.1
  130.3 2.8 %copy.20 = bf16[1,2048,384]{2,1,0:T(8,128)(2,1)} copy(bf16[1,2048,384]{2,1,0:T(8,128)(2,1)} %get-tuple-element.17) | data formatting | bytes 3145728
  133.1 0.0 copy-done.1
  133.1 0.0 copy-start
  133.1 1.1 copy.21
  134.3 0.8 copy-done
  135.1 1.1 copy.22
Async XLA Ops:
  130.3 2.8 %copy-start.1 = (bf16[1,2048,384]{2,1,0:T(8,128)(2,1)S(1)}, bf16[1,2048,384]{2,1,0:T(8,128)(2,1)}, u32[]{:S(2)}) copy-start(bf16[1,2048,384]{2,1,0:T(8,128)(2,1)} %get-tuple-element.18) | copy-start | bytes 4718596
  133.1 2.0 %copy-start = (bf16[1,384,2048]{2,1,0:T(8,128)(2,1)S(1)}, bf16[1,384,2048]{2,1,0:T(8,128)(2,1)}, u32[]{:S(2)}) copy-start(bf16[1,384,2048]{2,1,0:T(8,128)(2,1)} %get-tuple-element.19) | copy-start | bytes 4718596

commit v3 on v2

v3 whole, which is shorter than its diff:
```python
import functools
import math

import jax
import jax.numpy as jnp
from jax import lax
from jax.experimental import pallas as pl
from jax.experimental.pallas import tpu as pltpu
from jax.sharding import PartitionSpec as P

MESH = pl.DeviceIdType.MESH
F32, BF16 = jnp.float32, jnp.bfloat16
NT = (((1,), (1,)), ((), ()))
TN = (((0,), (0,)), ((), ()))


def dot(a, b, dims=(((1,), (0,)), ((), ()))):
    return lax.dot_general(a, b, dims, preferred_element_type=F32)


def quotient(x, n):
    return x >> (n.bit_length() - 1) if n & (n - 1) == 0 else x // n


def remainder(x, n):
    return x & (n - 1) if n & (n - 1) == 0 else lax.rem(x, n)


def tiles(count, body):
    def step(i, carry):
        body(i)
        return carry

    lax.fori_loop(0, count, step, 0)


def kernel(sizes, plan, back_plan, *refs):
    columns, rows, tokens, width, experts, units, top = sizes
    waves, returns = len(plan), len(back_plan)
    refs = list(refs)

    def take(count):
        taken, refs[:count] = refs[:count], []
        return taken

    tok_hbm, ups_hbm, probs, routes, wg_hbm, wu_hbm, wd_hbm = take(7)
    input_grad, prob_grad, gate_out, up_out, down_out = take(5)
    info, pick, pick_scaled, merge, wgu, wd, acc, acc_back, hidden, delta, named_by = take(11)
    ring, send, recv = take(waves), take(waves), take(waves)
    back_send, back_recv, row_send, row_recv = take(returns), take(returns), take(returns), take(returns)
    own_sem, weight_sem, ring_send_sem, ring_recv_sem, info_send_sem, info_recv_sem = take(6)
    send_sem, recv_sem, swap_send_sem, swap_recv_sem = take(4)
    back_send_sem, back_recv_sem, row_send_sem, row_recv_sem = take(4)

    reach = tokens * top // experts
    per_dest = rows * reach
    slots = columns * per_dest
    half = columns // 2
    side = math.isqrt(half)
    me_c, me_r = lax.axis_index("expert"), lax.axis_index("dp")
    core, me_y, me_x = lax.rem(me_c, 2), lax.rem(me_c // 2, side), me_c // (2 * side)
    pair, parity = me_r // 2, lax.rem(me_r, 2)
    partner = me_r + 1 - 2 * parity

    def row_at(offset):
        return lax.rem(me_r + (offset % rows), rows)

    def place_at(i):
        return lax.rem(me_x + i // side, side) * side + lax.rem(me_y + lax.rem(i, side), side)

    def column_at(i):
        return place_at(i // 2) * 2 + lax.rem(core + lax.rem(i, 2), 2)

    def block(column):
        slot = lax.rem(column, 2) * half + column // 2
        return pl.ds(pl.multiple_of(slot * per_dest, per_dest), per_dest)

    def core_half(number):
        return pl.ds(pl.multiple_of(number * (half * per_dest), half * per_dest), half * per_dest)

    own = block(me_c)
    others = (columns - 1) * per_dest

    def arrived(buffer, sem):
        pltpu.make_async_copy(buffer, buffer, sem).wait()

    own_copies = []
    for w in range(waves):
        kind, start, wide = plan[w][:3]
        source = (tok_hbm, ups_hbm)[kind].at[:, pl.ds(start, wide)]
        copy = pltpu.make_async_copy(source, ring[w].at[me_r], own_sem.at[w])
        copy.start()
        own_copies.append(copy)
    weight_copies = [
        pltpu.make_async_copy(wg_hbm.at[0], wgu.at[:, pl.ds(0, units)], weight_sem.at[0]),
        pltpu.make_async_copy(wu_hbm.at[0], wgu.at[:, pl.ds(units, units)], weight_sem.at[1]),
        pltpu.make_async_copy(wd_hbm.at[0], wd, weight_sem.at[2]),
    ]
    for copy in weight_copies:
        copy.start()

    barrier = pltpu.get_barrier_semaphore()

    def greet_column(i):
        pl.semaphore_signal(barrier, inc=1, device_id=(column_at(i + 1), me_r), device_id_type=MESH)

    tiles(columns - 1, greet_column)
    for offset in range(1, rows):
        pl.semaphore_signal(barrier, inc=1, device_id=(me_c, row_at(offset)), device_id_type=MESH)

    lane = lax.broadcasted_iota(jnp.int32, (tokens, experts), 1)
    named = jnp.zeros((tokens, experts), F32)
    weight = jnp.zeros((tokens, experts), F32)
    unit = lax.broadcasted_iota(jnp.int32, (top, top), 0) == lax.broadcasted_iota(jnp.int32, (top, top), 1)
    unit = jnp.where(unit, 1.0, 0.0).astype(BF16)
    named_by[...] = dot(routes[...].astype(F32).astype(BF16), unit, TN)
    probs_by = dot(probs[...], unit, TN)
    lane = lane.astype(F32)
    for k in range(top):
        hit = named_by[:, k : k + 1] == lane
        named = jnp.where(hit, 1.0, named)
        weight = jnp.where(hit, probs_by[:, k : k + 1], weight)
    upto = lax.broadcasted_iota(jnp.int32, (tokens, tokens), 0) >= lax.broadcasted_iota(jnp.int32, (tokens, tokens), 1)
    upto = jnp.where(upto, 1.0, 0.0).astype(BF16)
    rank = named * dot(upto, named.astype(BF16))
    info[me_r, 0:tokens, :] = rank.astype(BF16)
    info[me_r, tokens : 2 * tokens, :] = weight.astype(BF16)

    pl.semaphore_wait(barrier, columns - 1 + rows - 1)

    info_copies = []
    for offset in range(1, rows):
        copy = pltpu.make_async_remote_copy(
            info.at[me_r], info.at[me_r], info_send_sem.at[offset], info_recv_sem.at[offset],
            device_id=(me_c, row_at(offset)), device_id_type=MESH,
        )
        copy.start()
        info_copies.append(copy)

    span = [k for k in range(-((rows - 1) // 2), rows // 2 + 1) if k]
    near = [k for k in span if abs(k) <= 2]
    handed = [k for k in span if abs(k) > 2]

    def gather_copy(w, offset, via):
        sign = 1 if w % 2 == 0 else -1
        source = row_at(-sign * via)
        return pltpu.make_async_remote_copy(
            ring[w].at[source], ring[w].at[source], ring_send_sem.at[w, offset % rows], ring_recv_sem.at[w, offset % rows],
            device_id=(me_c, row_at(sign * (offset - via))), device_id_type=MESH,
        )

    def gather_arrived(w, offset):
        sign = 1 if w % 2 == 0 else -1
        source = row_at(-sign * offset)
        pltpu.make_async_remote_copy(
            ring[w].at[source], ring[w].at[source], ring_send_sem.at[w, offset % rows], ring_recv_sem.at[w, offset % rows],
            device_id=(me_c, row_at(sign * offset)), device_id_type=MESH,
        ).wait_recv()

    def via_of(offset):
        return 2 if offset > 0 else -2

    def make_picks():
        for offset in range(1, rows):
            source = row_at(-offset)
            pltpu.make_async_remote_copy(
                info.at[source], info.at[source], info_send_sem.at[offset], info_recv_sem.at[offset],
                device_id=(me_c, row_at(offset)), device_id_type=MESH,
            ).wait_recv()
        count = rows * tokens
        expert = lax.broadcasted_iota(jnp.int32, (experts, slots), 0)
        slot = quotient(lax.broadcasted_iota(jnp.int32, (experts, slots), 1), per_dest)
        column = remainder(slot, half) * 2 + quotient(slot, half)
        spread = jnp.where(expert == column * (rows // 2) + pair, 1.0, 0.0).astype(BF16)
        expert = lax.broadcasted_iota(jnp.int32, (slots, experts), 1)
        slot = quotient(lax.broadcasted_iota(jnp.int32, (slots, experts), 0), per_dest)
        column = remainder(slot, half) * 2 + quotient(slot, half)
        spread_t = jnp.where(expert == column * (rows // 2) + pair, 1.0, 0.0).astype(BF16)
        ranks_in = info[:, 0:tokens, :].reshape(count, experts)
        weights_in = info[:, tokens : 2 * tokens, :].reshape(count, experts)

        def matches(ranks, token, place):
            wanted = remainder(place, per_dest) - reach * quotient(token, tokens) + 1
            return (ranks > 0.5) & (ranks == wanted.astype(F32))

        shape = (slots, count)
        match = matches(
            dot(spread_t, ranks_in, NT), lax.broadcasted_iota(jnp.int32, shape, 1), lax.broadcasted_iota(jnp.int32, shape, 0)
        )
        pick[...] = jnp.where(match, 1.0, 0.0).astype(BF16)
        pick_scaled[...] = jnp.where(match, dot(spread_t, weights_in, NT), 0.0).astype(BF16)
        shape = (count, slots)
        match = matches(
            dot(ranks_in, spread), lax.broadcasted_iota(jnp.int32, shape, 0), lax.broadcasted_iota(jnp.int32, shape, 1)
        )
        merge[...] = jnp.where(match, 1.0, 0.0).astype(BF16)

    def tile_of(wide):
        return 256 if wide % 256 == 0 else 128

    def send_wave(w):
        kind, _, wide, split = plan[w][:4]
        chosen = pick if kind == 0 else pick_scaled
        tile = tile_of(wide)

        def one(i):
            at = pl.ds(pl.multiple_of(i * tile, tile), tile)
            send[w][:, at] = dot(chosen[...], ring[w][:, :, at].reshape(rows * tokens, tile)).astype(BF16)

        tiles(wide // tile, one)

        def ship(to):
            pltpu.make_async_remote_copy(
                send[w].at[block(to)], recv[w].at[own], send_sem.at[w], recv_sem.at[w],
                device_id=(to, me_r), device_id_type=MESH,
            ).start()

        if split:
            @pl.when(parity == 0)
            def _():
                pltpu.make_async_copy(send[w].at[own], recv[w].at[own], recv_sem.at[w]).start()

            def step(i, carry):
                ship(place_at(lax.rem(i * 5, half)) * 2 + lax.rem(core + parity, 2))
                return carry

            lax.fori_loop(1 - parity, half, step, 0)
        else:
            recv[w][own, :] = send[w][own, :]
            tiles(columns - 1, lambda i: ship(column_at(lax.rem((i + 1) * 11, columns))))

    served = lax.rem(core + parity, 2)

    def swap(w):
        return pltpu.make_async_remote_copy(
            recv[w].at[core_half(served)], recv[w].at[core_half(served)], swap_send_sem.at[w], swap_recv_sem.at[w],
            device_id=(me_c, partner), device_id_type=MESH,
        )

    unit_tile = tile_of(2 * units)
    back_tile = 128
    block_rows = 64
    swapping, projected = [], []

    def project(w):
        kind, start, wide = plan[w][:3]
        opens = all(plan[v][0] != kind for v in projected)

        def forward(i):
            at = pl.ds(pl.multiple_of(i * unit_tile, unit_tile), unit_tile)
            value = dot(recv[w][...], wgu[start : start + wide, at])
            acc[:, at] = value if opens else acc[:, at] + value

        def backward(i):
            at = pl.ds(pl.multiple_of(i * back_tile, back_tile), back_tile)
            value = dot(recv[w][...], wd[at, start : start + wide], NT)
            acc_back[:, at] = value if opens else acc_back[:, at] + value

        if kind == 0:
            tiles(2 * units // unit_tile, forward)
        else:
            tiles(units // back_tile, backward)

    def activate(i):
        at = pl.ds(pl.multiple_of(i * block_rows, block_rows), block_rows)
        gate, up = acc[at, 0:units], acc[at, units : 2 * units]
        sigmoid = jax.nn.sigmoid(gate)
        activation = gate * sigmoid
        hidden[at, :] = (activation * up).astype(BF16)
        acc[at, 0:units] = up * (sigmoid * (1.0 + gate * (1.0 - sigmoid)))
        acc[at, units : 2 * units] = activation

    def finish(w):
        if plan[w][3]:
            swap(w).wait_recv()
        project(w)
        projected.append(w)
        if plan[w][0] == 0 and all(v in projected for v in range(waves) if plan[v][0] == 0):
            tiles(slots // block_rows, activate)

    direct = [not handed or steps == 1 for *_, steps in plan]
    started = [max(0, w - lead) for w, (*_, lead, _) in enumerate(plan)]
    relayed = [min(w, started[w] + 1) for w in range(waves)]
    farthest = sorted(span, key=lambda k: -abs(k))
    for tick in range(waves + PACE):
        for w in range(waves):
            if tick == started[w]:
                own_copies[w].wait()
                for offset in farthest if direct[w] else sorted(near, key=lambda k: -abs(k)):
                    gather_copy(w, offset, 0).start()
        if tick == 0:
            make_picks()
        for w in range(waves):
            if tick == relayed[w] and not direct[w]:
                for via in sorted(set(via_of(offset) for offset in handed)):
                    gather_arrived(w, via)
                    for offset in handed:
                        if via_of(offset) == via:
                            gather_copy(w, offset, via).start()
        if tick < waves:
            for offset in span:
                if direct[tick] or offset in handed or all(via_of(other) != offset for other in handed):
                    gather_arrived(tick, offset)
        landed = tick - PACE
        if landed == 0:
            for copy in weight_copies:
                copy.wait()
        if landed >= 0:
            if plan[landed][3]:
                arrived(recv[landed].at[core_half(served)], recv_sem.at[landed])
                swap(landed).start()
                swapping.append(landed)
            else:
                arrived(recv[landed].at[pl.ds(0, others)], recv_sem.at[landed])
        if tick < waves:
            send_wave(tick)
        if landed >= 0 and not plan[landed][3]:
            finish(landed)
        while swapping and (swapping[0] <= landed - SWAP_LAG or landed == waves - 1):
            finish(swapping.pop(0))

    own_expert = me_c * (rows // 2) + pair

    def deltas(i):
        at = pl.ds(pl.multiple_of(i * block_rows, block_rows), block_rows)
        back = acc_back[at, :]
        delta[at, 0:units] = (back * acc[at, 0:units]).astype(BF16)
        delta[at, units : 2 * units] = (back * acc[at, units : 2 * units]).astype(BF16)
        partial = jnp.sum(hidden[at, :].astype(F32) * back, axis=1, keepdims=True)
        place = lax.broadcasted_iota(jnp.int32, (block_rows, experts), 1)
        mark = back_plan[MARKED][1]
        back_send[MARKED][at, mark : mark + experts] = jnp.where(place == own_expert, partial, 0.0).astype(BF16)

    tiles(slots // block_rows, deltas)

    def send_back(v):
        start, wide = back_plan[v]
        part_tile = tile_of(wide)

        def term(i):
            at = pl.ds(pl.multiple_of(i * part_tile, part_tile), part_tile)
            from_row = pl.ds(pl.multiple_of(start + i * part_tile, part_tile), part_tile)
            back_send[v][:, at] = dot(delta[...], wgu[from_row, :], NT).astype(BF16)

        tiles(wide // part_tile, term)
        back_recv[v][own, :] = back_send[v][own, :]

        def ship_back(i):
            to = column_at(lax.rem((i + 1) * 11, columns))
            pltpu.make_async_remote_copy(
                back_send[v].at[block(to)], back_recv[v].at[own], back_send_sem.at[v], back_recv_sem.at[v],
                device_id=(to, me_r), device_id_type=MESH,
            ).start()

        tiles(columns - 1, ship_back)

    def weight_gradients(w):
        kind, start, wide = plan[w][:3]
        tile = tile_of(wide)

        def gate_up(i):
            at = pl.ds(pl.multiple_of(i * tile, tile), tile)
            to = pl.ds(pl.multiple_of(start + i * tile, tile), tile)
            value = dot(recv[w][:, at], delta[...], TN).astype(BF16)
            gate_out[0, to, :] = value[:, 0:units]
            up_out[0, to, :] = value[:, units : 2 * units]

        def down(i):
            at = pl.ds(pl.multiple_of(i * tile, tile), tile)
            to = pl.ds(pl.multiple_of(start + i * tile, tile), tile)
            down_out[0, :, to] = dot(hidden[...], recv[w][:, at], TN).astype(BF16)

        tiles(wide // tile, gate_up if kind == 0 else down)

    def combine(v):
        arrived(back_recv[v].at[pl.ds(0, others)], back_recv_sem.at[v])
        summed = dot(merge[...], back_recv[v][...]).astype(BF16).reshape(row_send[v].shape)
        row_send[v][...] = summed
        row_recv[v][me_r] = row_send[v][me_r]
        for offset in range(1, rows):
            to = row_at(offset)
            pltpu.make_async_remote_copy(
                row_send[v].at[to], row_recv[v].at[me_r], row_send_sem.at[v], row_recv_sem.at[v],
                device_id=(me_c, to), device_id_type=MESH,
            ).start()

    done = 0
    for v in range(min(WINDOW, returns)):
        send_back(v)
    for v in range(returns):
        while done < waves and done * returns <= (v + 1) * waves:
            weight_gradients(done)
            done = done + 1
        combine(v)
        if v + WINDOW < returns:
            send_back(v + WINDOW)

    for v in range(returns):
        start, wide = back_plan[v]
        arrived(row_recv[v].at[pl.ds(0, rows - 1)], row_recv_sem.at[v])
        total = row_recv[v][0].astype(F32)
        for r in range(1, rows):
            total = total + row_recv[v][r].astype(F32)
        input_grad[:, start : start + wide] = total[:, 0:wide].astype(BF16)
        if v == MARKED:
            partials = total[:, wide : wide + experts]
            place = lax.broadcasted_iota(jnp.int32, (tokens, top), 1)
            result = jnp.zeros((tokens, top), F32)
            for k in range(top):
                own_value = jnp.sum(jnp.where(named_by[:, k : k + 1] == lane, partials, 0.0), axis=1, keepdims=True)
                result = jnp.where(place == k, own_value / probs_by[:, k : k + 1], result)
            token_unit = lax.broadcasted_iota(jnp.int32, (tokens, tokens), 0) == lax.broadcasted_iota(jnp.int32, (tokens, tokens), 1)
            prob_grad[...] = dot(result.astype(BF16), jnp.where(token_unit, 1.0, 0.0).astype(BF16), TN)

    for copy in info_copies:
        copy.wait_send()
    for w in range(waves):
        for offset in span:
            gather_copy(w, offset, via_of(offset) if offset in handed and not direct[w] else 0).wait_send()
        if plan[w][3]:
            swap(w).wait_send()
            served_rows = (half - 1) * per_dest
            if served_rows:
                arrived(send[w].at[pl.ds(0, served_rows)], send_sem.at[w])

            @pl.when(parity == 1)
            def _():
                arrived(send[w].at[pl.ds(0, per_dest)], send_sem.at[w])
        else:
            arrived(send[w].at[pl.ds(0, others)], send_sem.at[w])
    for v in range(returns):
        arrived(back_send[v].at[pl.ds(0, others)], back_send_sem.at[v])
        arrived(row_send[v].at[pl.ds(0, rows - 1)], row_send_sem.at[v])


def local(plan, back_plan, tokens, upstream, gate_probs, routes, w_gate, w_up, w_down):
    columns, rows = lax.axis_size("expert"), lax.axis_size("dp")
    count, width = tokens.shape
    top = routes.shape[1]
    units = w_gate.shape[2]
    experts = columns * rows // 2
    slots = columns * rows * (count * top // experts)
    waves, returns = len(plan), len(back_plan)
    wides = [wave[2] for wave in plan]
    backs = [wide + (experts if v == MARKED else 0) for v, (_, wide) in enumerate(back_plan)]
    dma = pltpu.SemaphoreType.DMA
    any_space, vmem = pl.BlockSpec(memory_space=pl.ANY), pl.BlockSpec(memory_space=pltpu.VMEM)
    input_grad, prob_grad, gate_grad, up_grad, down_grad = pl.pallas_call(
        functools.partial(kernel, (columns, rows, count, width, experts, units, top), plan, back_plan),
        out_shape=[
            pltpu.VMEM((count, width), BF16),
            pltpu.VMEM((top, count), F32),
            pltpu.VMEM(w_gate.shape, BF16),
            pltpu.VMEM(w_up.shape, BF16),
            pltpu.VMEM(w_down.shape, BF16),
        ],
        in_specs=[any_space, any_space, vmem, vmem, any_space, any_space, any_space],
        out_specs=[vmem] * 5,
        scratch_shapes=[
            pltpu.VMEM((rows, 2 * count, experts), BF16),
            pltpu.VMEM((slots, rows * count), BF16),
            pltpu.VMEM((slots, rows * count), BF16),
            pltpu.VMEM((rows * count, slots), BF16),
            pltpu.VMEM((width, 2 * units), BF16),
            pltpu.VMEM((units, width), BF16),
            pltpu.VMEM((slots, 2 * units), F32),
            pltpu.VMEM((slots, units), F32),
            pltpu.VMEM((slots, units), BF16),
            pltpu.VMEM((slots, 2 * units), BF16),
            pltpu.VMEM((count, top), F32),
        ]
        + [pltpu.VMEM((rows, count, wide), BF16) for wide in wides]
        + [pltpu.VMEM((slots, wide), BF16) for wide in wides] * 2
        + [pltpu.VMEM((slots, wide), BF16) for wide in backs] * 2
        + [pltpu.VMEM((rows, count, wide), BF16) for wide in backs] * 2
        + [
            dma((waves,)),
            dma((3,)),
            dma((waves, rows)),
            dma((waves, rows)),
            dma((rows,)),
            dma((rows,)),
            dma((waves,)),
            dma((waves,)),
            dma((waves,)),
            dma((waves,)),
            dma((returns,)),
            dma((returns,)),
            dma((returns,)),
            dma((returns,)),
        ],
        compiler_params=pltpu.CompilerParams(
            collective_id=0, has_side_effects=True, vmem_limit_bytes=48 * 1024 * 1024
        ),
        cost_estimate=pl.CostEstimate(
            flops=16 * slots * width * units, bytes_accessed=24 * width * units, transcendentals=slots * units
        ),
    )(tokens, upstream, gate_probs.T, routes.T, w_gate, w_up, w_down)
    return input_grad, prob_grad.T, gate_grad, up_grad, down_grad


PLAN = (
    (0, 0, 1, 0, 4, 1),
    (0, 1, 1, 0, 4, 2),
    (0, 2, 2, 1, 4, 2),
    (0, 4, 2, 1, 4, 2),
    (0, 6, 2, 1, 4, 2),
    (1, 0, 2, 1, 4, 2),
    (1, 2, 2, 0, 4, 2),
    (1, 4, 2, 0, 4, 2),
    (1, 6, 2, 0, 4, 2),
)
PACE, SWAP_LAG = 3, 2
BACK_PLAN = ((0, 1), (1, 1), (2, 2), (4, 2), (6, 1), (7, 1))
MARKED = 1
WINDOW = 3


def solution(mesh):
    both = ("expert", "dp")
    flat, deep = P(both, None), P(both, None, None)

    def whole(tokens, *others):
        unit = tokens.shape[1] // 8
        plan = tuple((kind, start * unit, wide * unit, bool(split), *rest) for kind, start, wide, split, *rest in PLAN)
        back_plan = tuple((start * unit, wide * unit) for start, wide in BACK_PLAN)
        return jax.shard_map(
            functools.partial(local, plan, back_plan),
            mesh=mesh,
            in_specs=(flat, flat, flat, flat, deep, deep, deep),
            out_specs=(flat, flat, deep, deep, deep),
            check_vma=False,
        )(tokens, *others)

    return whole
```

time: 137 us -> 119 us (0.87)
  Pallas kernels: 124 us -> 111 us
  local copies, waits for them, and re-layouts: 11.6 us -> 7.84 us
    pallas_call x1, Pallas kernels: 124 us -> 111 us  [local(): pl.pallas_call(functools.partial(kernel, (columns, rows, count, width, ex...]
    unnamed x10 -> x13, local copies, waits for them, and re-layouts: 10.2 us -> 7.84 us
    pallas_call x1 -> x0, local copies, waits for them, and re-layouts: 1.38 us -> none  [local(): pl.pallas_call(functools.partial(kernel, (columns, rows, count, width, ex...]
where the time goes in v3:
time: 119 us
  Pallas kernels  111 us (93%)
  local copies, waits for them, and re-layouts  7.84 us (7%)
    pallas_call x1, Pallas kernels, local(): pl.pallas_call(functools.partial(kernel, (columns, rows, count, width, ex...  111 us
    unnamed x13, local copies, waits for them, and re-layouts  7.84 us

profile of v3, /device:TPU:1, one launch (start us, length us, event | category | flops | bytes accessed | tf_op | source)
XLA Modules:
  0.0 119.3 jit_solution(16689396072166341825)
XLA Ops:
  0.6 0.0 copy-start
  0.6 0.9 copy-done
  1.5 0.0 copy-start.1
  1.5 0.9 copy-done.1
  2.4 0.0 copy-start.2
  2.4 0.7 copy-done.2
  3.1 0.0 copy-start.3
  3.1 0.7 copy-done.3
  3.8 110.8 %shard_map.110 = (bf16[32,2048]{1,0:T(8,128)(2,1)S(1)}, f32[8,32]{1,0:T(8,128)S(1)}, bf16[1,2048,384]{2,1,0:T(8,128)(2,1)S(1)}, bf16[1,2048,384]{2,1,0:T(8,128)(2,1)S(1)}, bf16[1,384,2048]{2,1,0:T(8,128)(2,1)S(1)}) custom-call(bf16[32,2048]{1,0:T(8,128)(2,1)S(1)} %copy-done, bf16[32,2048]{1,0:T(8,128)(2,1)S(1)} %copy-done.1, bf16[8,32]{1,0:T(8,128)(2,1)S(1)} %bitcast.5, ...), custom_call_target="tpu_custom_call" | custom-call | flops 6442450944 | bytes 18874368 | tf_op jit(solution)/shard_map/pallas_call | solution.py:448
  114.6 0.7 copy.17
  115.3 0.6 copy.18
  115.9 1.1 copy.19
  117.0 1.1 copy.20
  118.2 1.1 copy.21
Async XLA Ops:
  0.6 0.9 copy-start
  1.5 0.9 copy-start.1
  2.4 0.7 copy-start.2
  3.1 0.7 copy-start.3

commit v4 on v3

--- a/solution.py
+++ b/solution.py
@@ -43,9 +43,9 @@
         taken, refs[:count] = refs[:count], []
         return taken
 
-    tok_hbm, ups_hbm, probs, routes, wg_hbm, wu_hbm, wd_hbm = take(7)
+    tok_hbm, ups_hbm, probs_hbm, routes_hbm, wg_hbm, wu_hbm, wd_hbm = take(7)
     input_grad, prob_grad, gate_out, up_out, down_out = take(5)
-    info, pick, pick_scaled, merge, wgu, wd, acc, acc_back, hidden, delta, named_by = take(11)
+    info, pick, pick_scaled, merge, wgu, wd, acc, acc_back, hidden, delta, named_by, probs, routes = take(13)
     ring, send, recv = take(waves), take(waves), take(waves)
     back_send, back_recv, row_send, row_recv = take(returns), take(returns), take(returns), take(returns)
     own_sem, weight_sem, ring_send_sem, ring_recv_sem, info_send_sem, info_recv_sem = take(6)
@@ -91,6 +91,12 @@
         copy = pltpu.make_async_copy(source, ring[w].at[me_r], own_sem.at[w])
         copy.start()
         own_copies.append(copy)
+    route_copies = [
+        pltpu.make_async_copy(probs_hbm, probs, weight_sem.at[3]),
+        pltpu.make_async_copy(routes_hbm, routes, weight_sem.at[4]),
+    ]
+    for copy in route_copies:
+        copy.start()
     weight_copies = [
         pltpu.make_async_copy(wg_hbm.at[0], wgu.at[:, pl.ds(0, units)], weight_sem.at[0]),
         pltpu.make_async_copy(wu_hbm.at[0], wgu.at[:, pl.ds(units, units)], weight_sem.at[1]),
@@ -107,6 +113,9 @@
     tiles(columns - 1, greet_column)
     for offset in range(1, rows):
         pl.semaphore_signal(barrier, inc=1, device_id=(me_c, row_at(offset)), device_id_type=MESH)
+
+    for copy in route_copies:
+        copy.wait()
 
     lane = lax.broadcasted_iota(jnp.int32, (tokens, experts), 1)
     named = jnp.zeros((tokens, experts), F32)
@@ -138,8 +147,16 @@
         info_copies.append(copy)
 
     span = [k for k in range(-((rows - 1) // 2), rows // 2 + 1) if k]
-    near = [k for k in span if abs(k) <= 2]
-    handed = [k for k in span if abs(k) > 2]
+
+    def via_of(w, offset):
+        steps, way = plan[w][5], 1 if offset > 0 else -1
+        if steps == 1 or abs(offset) <= (2 if steps == 2 else 1):
+            return 0
+        return 2 * way if steps == 2 else offset - way
+
+    def stage_of(w, offset):
+        via = via_of(w, offset)
+        return 0 if via == 0 else stage_of(w, via) + 1
 
     def gather_copy(w, offset, via):
         sign = 1 if w % 2 == 0 else -1
@@ -156,9 +173,6 @@
             ring[w].at[source], ring[w].at[source], ring_send_sem.at[w, offset % rows], ring_recv_sem.at[w, offset % rows],
             device_id=(me_c, row_at(sign * offset)), device_id_type=MESH,
         ).wait_recv()
-
-    def via_of(offset):
-        return 2 if offset > 0 else -2
 
     def make_picks():
         for offset in range(1, rows):
@@ -278,29 +292,33 @@
         if plan[w][0] == 0 and all(v in projected for v in range(waves) if plan[v][0] == 0):
             tiles(slots // block_rows, activate)
 
-    direct = [not handed or steps == 1 for *_, steps in plan]
-    started = [max(0, w - lead) for w, (*_, lead, _) in enumerate(plan)]
-    relayed = [min(w, started[w] + 1) for w in range(waves)]
+    started = [start for *_, start, _ in plan]
+    heard = set()
+
+    def hear(w, offset):
+        if (w, offset) not in heard:
+            heard.add((w, offset))
+            gather_arrived(w, offset)
+
     farthest = sorted(span, key=lambda k: -abs(k))
     for tick in range(waves + PACE):
         for w in range(waves):
-            if tick == started[w]:
-                own_copies[w].wait()
-                for offset in farthest if direct[w] else sorted(near, key=lambda k: -abs(k)):
-                    gather_copy(w, offset, 0).start()
+            for stage in range(rows):
+                if tick != min(w, started[w] + stage):
+                    continue
+                if stage == 0:
+                    own_copies[w].wait()
+                for offset in farthest:
+                    if stage_of(w, offset) == stage:
+                        via = via_of(w, offset)
+                        if via:
+                            hear(w, via)
+                        gather_copy(w, offset, via).start()
         if tick == 0:
             make_picks()
-        for w in range(waves):
-            if tick == relayed[w] and not direct[w]:
-                for via in sorted(set(via_of(offset) for offset in handed)):
-                    gather_arrived(w, via)
-                    for offset in handed:
-                        if via_of(offset) == via:
-                            gather_copy(w, offset, via).start()
         if tick < waves:
             for offset in span:
-                if direct[tick] or offset in handed or all(via_of(other) != offset for other in handed):
-                    gather_arrived(tick, offset)
+                hear(tick, offset)
         landed = tick - PACE
         if landed == 0:
             for copy in weight_copies:
@@ -416,7 +434,7 @@
         copy.wait_send()
     for w in range(waves):
         for offset in span:
-            gather_copy(w, offset, via_of(offset) if offset in handed and not direct[w] else 0).wait_send()
+            gather_copy(w, offset, via_of(w, offset)).wait_send()
         if plan[w][3]:
             swap(w).wait_send()
             served_rows = (half - 1) * per_dest
@@ -444,7 +462,7 @@
     wides = [wave[2] for wave in plan]
     backs = [wide + (experts if v == MARKED else 0) for v, (_, wide) in enumerate(back_plan)]
     dma = pltpu.SemaphoreType.DMA
-    any_space, vmem = pl.BlockSpec(memory_space=pl.ANY), pl.BlockSpec(memory_space=pltpu.VMEM)
+    hbm, vmem = pl.BlockSpec(memory_space=pltpu.HBM), pl.BlockSpec(memory_space=pltpu.VMEM)
     input_grad, prob_grad, gate_grad, up_grad, down_grad = pl.pallas_call(
         functools.partial(kernel, (columns, rows, count, width, experts, units, top), plan, back_plan),
         out_shape=[
@@ -454,7 +472,7 @@
             pltpu.VMEM(w_up.shape, BF16),
             pltpu.VMEM(w_down.shape, BF16),
         ],
-        in_specs=[any_space, any_space, vmem, vmem, any_space, any_space, any_space],
+        in_specs=[hbm] * 7,
         out_specs=[vmem] * 5,
         scratch_shapes=[
             pltpu.VMEM((rows, 2 * count, experts), BF16),
@@ -468,6 +486,8 @@
             pltpu.VMEM((slots, units), BF16),
             pltpu.VMEM((slots, 2 * units), BF16),
             pltpu.VMEM((count, top), F32),
+            pltpu.VMEM((top, count), BF16),
+            pltpu.VMEM((top, count), jnp.int32),
         ]
         + [pltpu.VMEM((rows, count, wide), BF16) for wide in wides]
         + [pltpu.VMEM((slots, wide), BF16) for wide in wides] * 2
@@ -475,7 +495,7 @@
         + [pltpu.VMEM((rows, count, wide), BF16) for wide in backs] * 2
         + [
             dma((waves,)),
-            dma((3,)),
+            dma((5,)),
             dma((waves, rows)),
             dma((waves, rows)),
             dma((rows,)),
@@ -500,20 +520,20 @@
 
 
 PLAN = (
-    (0, 0, 1, 0, 4, 1),
-    (0, 1, 1, 0, 4, 2),
-    (0, 2, 2, 1, 4, 2),
-    (0, 4, 2, 1, 4, 2),
-    (0, 6, 2, 1, 4, 2),
-    (1, 0, 2, 1, 4, 2),
-    (1, 2, 2, 0, 4, 2),
-    (1, 4, 2, 0, 4, 2),
-    (1, 6, 2, 0, 4, 2),
+    (0, 0, 1, 0, 0, 1),
+    (0, 1, 1, 0, 0, 2),
+    (0, 2, 2, 0, 0, 2),
+    (0, 4, 2, 1, 0, 2),
+    (0, 6, 2, 1, 1, 2),
+    (1, 0, 2, 1, 1, 4),
+    (1, 2, 2, 0, 2, 4),
+    (1, 4, 2, 0, 3, 4),
+    (1, 6, 2, 0, 4, 4),
 )
 PACE, SWAP_LAG = 3, 2
-BACK_PLAN = ((0, 1), (1, 1), (2, 2), (4, 2), (6, 1), (7, 1))
+BACK_PLAN = tuple((start, 1) for start in range(8))
 MARKED = 1
-WINDOW = 3
+WINDOW = 4
 
 
 def solution(mesh):

time: 119 us -> 115 us (0.966)
  Pallas kernels: 111 us -> 106 us
    pallas_call x1, Pallas kernels: 111 us -> 106 us  [local(): pl.pallas_call(functools.partial(kernel, (columns, rows, count, width, ex...]
where the time goes in v4:
time: 115 us
  Pallas kernels  106 us (92%)
  local copies, waits for them, and re-layouts  7.84 us (7%)
    pallas_call x1, Pallas kernels, local(): pl.pallas_call(functools.partial(kernel, (columns, rows, count, width, ex...  106 us
    unnamed x13, local copies, waits for them, and re-layouts  7.84 us

profile of v4, /device:TPU:1, one launch (start us, length us, event | category | flops | bytes accessed | tf_op | source)
XLA Modules:
  0.0 114.7 jit_solution(10478382830480911727)
XLA Ops:
  0.6 0.0 copy-start
  0.6 0.9 copy-done
  1.5 0.0 copy-start.1
  1.5 0.9 copy-done.1
  2.4 0.0 copy-start.2
  2.4 0.7 copy-done.2
  3.1 0.0 copy-start.3
  3.1 0.7 copy-done.3
  3.8 106.2 %shard_map.110 = (bf16[32,2048]{1,0:T(8,128)(2,1)S(1)}, f32[8,32]{1,0:T(8,128)S(1)}, bf16[1,2048,384]{2,1,0:T(8,128)(2,1)S(1)}, bf16[1,2048,384]{2,1,0:T(8,128)(2,1)S(1)}, bf16[1,384,2048]{2,1,0:T(8,128)(2,1)S(1)}) custom-call(bf16[32,2048]{1,0:T(8,128)(2,1)S(1)} %copy-done, bf16[32,2048]{1,0:T(8,128)(2,1)S(1)} %copy-done.1, bf16[8,32]{1,0:T(8,128)(2,1)S(1)} %bitcast.5, ...), custom_call_target="tpu_custom_call" | custom-call | flops 6442450944 | bytes 18874368 | tf_op jit(solution)/shard_map/pallas_call | solution.py:466
  110.0 0.7 copy.17
  110.7 0.6 copy.18
  111.3 1.1 copy.19
  112.4 1.1 copy.20
  113.6 1.1 copy.21
Async XLA Ops:
  0.6 0.9 copy-start
  1.5 0.9 copy-start.1
  2.4 0.7 copy-start.2
  3.1 0.7 copy-start.3

commit v5 on v4

--- a/solution.py
+++ b/solution.py
@@ -510,7 +510,7 @@
             dma((returns,)),
         ],
         compiler_params=pltpu.CompilerParams(
-            collective_id=0, has_side_effects=True, vmem_limit_bytes=48 * 1024 * 1024
+            collective_id=0, has_side_effects=True, vmem_limit_bytes=58 * 1024 * 1024
         ),
         cost_estimate=pl.CostEstimate(
             flops=16 * slots * width * units, bytes_accessed=24 * width * units, transcendentals=slots * units

time: 115 us -> 112 us (0.974)
  local copies, waits for them, and re-layouts: 7.84 us -> 4.68 us
    unnamed x13 -> x5, local copies, waits for them, and re-layouts: 7.84 us -> 4.68 us
where the time goes in v5:
time: 112 us
  Pallas kernels  106 us (95%)
  local copies, waits for them, and re-layouts  4.68 us (4%)
    pallas_call x1, Pallas kernels, local(): pl.pallas_call(functools.partial(kernel, (columns, rows, count, width, ex...  106 us
    unnamed x5, local copies, waits for them, and re-layouts  4.68 us

profile of v5, /device:TPU:1, one launch (start us, length us, event | category | flops | bytes accessed | tf_op | source)
XLA Modules:
  0.0 111.5 jit_solution(9900767113158415920)
XLA Ops:
  0.6 106.2 %shard_map.110 = (bf16[32,2048]{1,0:T(8,128)(2,1)S(1)}, f32[8,32]{1,0:T(8,128)S(1)}, bf16[1,2048,384]{2,1,0:T(8,128)(2,1)S(1)}, bf16[1,2048,384]{2,1,0:T(8,128)(2,1)S(1)}, bf16[1,384,2048]{2,1,0:T(8,128)(2,1)S(1)}) custom-call(bf16[32,2048]{1,0:T(8,128)(2,1)} %refs_0_.1, bf16[32,2048]{1,0:T(8,128)(2,1)} %refs_1_.1, bf16[8,32]{1,0:T(8,128)(2,1)} %bitcast.5, ...), custom_call_target="tpu_custom_call" | custom-call | flops 6442450944 | bytes 18874368 | tf_op jit(solution)/shard_map/pallas_call | solution.py:466
  106.8 0.7 copy.17
  107.5 0.6 copy.18
  108.1 1.1 %copy.19 = bf16[1,2048,384]{2,1,0:T(8,128)(2,1)} copy(bf16[1,2048,384]{2,1,0:T(8,128)(2,1)S(1)} %get-tuple-element.17) | data formatting | bytes 3145728
  109.2 1.1 %copy.20 = bf16[1,2048,384]{2,1,0:T(8,128)(2,1)} copy(bf16[1,2048,384]{2,1,0:T(8,128)(2,1)S(1)} %get-tuple-element.18) | data formatting | bytes 3145728
  110.4 1.1 %copy.21 = bf16[1,384,2048]{2,1,0:T(8,128)(2,1)} copy(bf16[1,384,2048]{2,1,0:T(8,128)(2,1)S(1)} %get-tuple-element.19) | data formatting | bytes 3145728
